TPU v7x, 32 devices: a whole 2x2x4 slice. The times are simulated.
32 devices in a mesh: expert: 8 (over y, x, core), hidden: 4 (over z).
Axes of the slice: x: 2, y: 2, z: 4, core: 2. Of those that a mesh axis runs over, the one named last changes fastest.
Arguments:
- cotangent: bfloat16 [8192, 2048], P(('expert', 'hidden')), may hold values from -6 to 6
- slot_token: int32 [32, 8, 80], P(('expert', 'hidden')), may hold values from -1 to 255, as said below
- slot_gate: float32 [32, 8, 80], P(('expert', 'hidden')), may hold values from 0.1 to 1
- w_down: bfloat16 [8, 4096, 2048], P('expert', 'hidden'), may hold values from -0.09375 to 0.09375
Outputs:
- hidden_grad: bfloat16 [8, 2048, 4096], P('expert', None, 'hidden')
Inputs may be any that keep to these rules, and one draw needn't show every extreme that they name: `slot_token`: on each device and for each expert the live slots come first and name distinct local tokens; a device fills at most 80 slots for one expert. For each expert and each index of the hidden axis, the 8 devices with that index name exactly 512 tokens together, so each expert takes exactly 2048 tokens.
All inputs are finite; a program needn't handle non-finite values.
Results may differ from a plain program's by a relative error of at most 0.0049.
Values may be sent and summed in bfloat16 or wider, within the bound.
A program may use at most 128 MiB of HBM per device.

v0:
```python
import jax
import jax.numpy as jnp
from jax import lax
from jax.sharding import PartitionSpec as P

CF = 2


def pick_live(flat_rows, slot_count, slot_width, row_total):
    running = jnp.cumsum(slot_count).astype(jnp.int32)
    first_slot = running - slot_count
    row_number = jnp.arange(row_total, dtype=jnp.int32)
    source = jnp.sum((running[None, :] <= row_number[:, None]).astype(jnp.int32), axis=1)
    flat_index = source * slot_width + row_number - first_slot[source]
    return flat_rows[flat_index]


def shards(cotangent, slot_token, slot_gate, w_down):
    slot_index = slot_token[0]
    live_slot = slot_index >= 0
    gate_value = jnp.where(live_slot, slot_gate[0], jnp.float32(0.0))
    token_rows = cotangent[jnp.maximum(slot_index, 0)]
    scaled = (gate_value[:, :, None] * token_rows.astype(jnp.float32)).astype(jnp.bfloat16)
    slot_count = jnp.sum(live_slot.astype(jnp.int32), axis=1)
    arrived, arrived_counts = (
        lax.all_to_all(scaled, "expert", split_axis=0, concat_axis=0, tiled=True),
        lax.all_to_all(slot_count, "expert", split_axis=0, concat_axis=0, tiled=True),
    )
    weight = w_down[0]
    slot_width = arrived.shape[1]
    feature_count = arrived.shape[2]
    group_rows = CF * cotangent.shape[0]
    compact = pick_live(arrived.reshape(-1, feature_count), arrived_counts, slot_width, group_rows)
    result = jnp.einsum(
        "rd,fd->rf",
        lax.all_gather(compact, "hidden", axis=0, tiled=True),
        weight,
        preferred_element_type=jnp.float32,
    ).astype(jnp.bfloat16)
    return result[None]


def solution(mesh):
    in_specs = (
        P(("expert", "hidden"), None),
        P(("expert", "hidden"), None, None),
        P(("expert", "hidden"), None, None),
        P("expert", "hidden", None),
    )
    out_specs = P("expert", None, "hidden")
    return jax.shard_map(shards, mesh=mesh, in_specs=in_specs, out_specs=out_specs, check_vma=False)
```

profile of v0, /device:TPU:0, one launch (start us, length us, event | category | flops | bytes accessed | tf_op | source)
XLA Modules:
  0.0 235.7 jit_solution(10478427980893430705)
XLA Ops:
  6.5 0.0 copy-start
  6.5 0.9 convert_reduce_fusion.1
  7.4 0.7 copy.7
  8.1 5.2 %all-to-all-start.1 = ((s32[8,1,1]{2,1,0:T(1,128)}), s32[8,1,1]{2,1,0:T(1,128)S(1)}, u32[]{:S(2)}, u32[]{:S(2)}) async-start(s32[8,1,1]{2,1,0:T(1,128)} %copy.7), calls=%async_computation.1 | async-start | bytes 8192 | tf_op jit(solution)/shard_map/all_to_all | solution.py:27
  13.3 0.1 reshape.104
  13.4 0.7 select_bitcast_fusion
  14.1 0.0 copy-done
  14.1 4.1 %gather_fusion = bf16[640,2048]{1,0:T(8,128)(2,1)} fusion(bf16[256,2048]{1,0:T(8,128)(2,1)S(1)} %copy-done, s32[1024]{0:T(1024)S(1)} %pad_clamp_fusion.1), kind=kCustom, calls=%fused_computation | custom fusion | bytes 5245440 | tf_op jit(solution)/shard_map/gather | solution.py:22
  18.1 3.7 %fusion = bf16[8,80,2048]{2,1,0:T(8,128)(2,1)} fusion(bf16[8,80,2048]{2,1,0:T(8,128)(2,1)} %bitcast.29, f32[8,80]{1,0:T(8,128)S(1)} %select_bitcast_fusion), kind=kLoop, calls=%fused_computation.3 | loop fusion | flops 3932160 | bytes 5245440 | tf_op jit(solution)/shard_map/convert_element_type | solution.py:23
  21.8 0.0 all-to-all-done.1
  21.8 4.4 %all-to-all-start = ((bf16[8,80,2048]{2,1,0:T(8,128)(2,1)}), bf16[8,80,2048]{2,1,0:T(8,128)(2,1)}, u32[]{:S(2)}, u32[]{:S(2)}) async-start(bf16[8,80,2048]{2,1,0:T(8,128)(2,1)} %fusion), calls=%async_computation | async-start | bytes 5242880 | tf_op jit(solution)/shard_map/all_to_all | solution.py:26
  26.2 0.0 all-gather.3.cloned.1.call-start
  26.3 0.2 reduce.1
  26.5 0.2 reduce-window.8
  26.7 0.7 fusion.5
  27.4 0.1 convert_reduce_fusion
  27.5 4.6 %compare_select_fusion.2 = s32[512,1]{0,1:T(1,128)S(1)} fusion(s32[]{:T(128)} %bitcast.7, s32[]{:T(128)} %bitcast.8, s32[]{:T(128)} %bitcast.9, s32[]{:T(128)} %bitcast.10, s32[]{:T(128)} %bitcast.11, s32[]{:T(128)} %bitcast.13, s32[]{:T(128)} %bitcast.12, s32[512,1]{0,1:T(1,128)S(1)} %bitcast.31), kind=kLoop, calls=%fused_computation.12 | loop fusion | flops 7680 | bytes 4124 | tf_op jit(solution)/shard_map/gather | solution.py:14
  32.1 0.6 broadcast_select_fusion
  32.8 25.8 %all-to-all-done = bf16[8,80,2048]{2,1,0:T(8,128)(2,1)} async-done(((bf16[8,80,2048]{2,1,0:T(8,128)(2,1)}), bf16[8,80,2048]{2,1,0:T(8,128)(2,1)}, u32[]{:S(2)}, u32[]{:S(2)}) %all-to-all-start) | async-done | bytes 2621472 | tf_op jit(solution)/shard_map/all_to_all | solution.py:26
  58.5 7.3 %gather_fusion.1 = bf16[512,2048]{1,0:T(8,128)(2,1)} fusion(bf16[640,2048]{1,0:T(8,128)(2,1)} %bitcast.2, s32[1024]{0:T(1024)S(1)} %pad_clamp_fusion), kind=kCustom, calls=%fused_computation.1 | custom fusion | bytes 4196352 | tf_op jit(solution)/shard_map/gather | solution.py:15
  65.8 0.0 all-gather.3.cloned.1.call-update
  65.8 149.2 %all-gather.3.cloned.1.call-done = bf16[2048,2048]{1,0:T(8,128)(2,1)} async-done(((bf16[512,2048]{1,0:T(8,128)(2,1)}), bf16[2048,2048]{1,0:T(8,128)(2,1)}) %all-gather.3.cloned.1.call-update) | async-done | bytes 8388624 | tf_op jit(solution)/shard_map/all_gather | solution.py:36
  215.0 13.9 %convert_bitcast_fusion = bf16[1,2048,1024]{2,1,0:T(8,128)(2,1)} fusion(bf16[2048,2048]{1,0:T(8,128)(2,1)} %all-gather.3.cloned.1.call-done, bf16[1,1024,2048]{2,1,0:T(8,128)(2,1)} %param.7), kind=kOutput, calls=%fused_computation.6 | convolution fusion | flops 8592031744 | bytes 16777216 | tf_op jit(solution)/shard_map/rd,fd->rf/dot_general | solution.py:34
  (5 shorter events, 0.1 us)
Async XLA Ops:
  6.5 7.5 %copy-start = (bf16[256,2048]{1,0:T(8,128)(2,1)S(1)}, bf16[256,2048]{1,0:T(8,128)(2,1)}, u32[]{:S(2)}) copy-start(bf16[256,2048]{1,0:T(8,128)(2,1)} %param.4) | copy-start | bytes 3145732
  8.1 13.7 %all-to-all-start.1 = ((s32[8,1,1]{2,1,0:T(1,128)}), s32[8,1,1]{2,1,0:T(1,128)S(1)}, u32[]{:S(2)}, u32[]{:S(2)}) async-start(s32[8,1,1]{2,1,0:T(1,128)} %copy.7), calls=%async_computation.1 | async-start | bytes 8192 | tf_op jit(solution)/shard_map/all_to_all | solution.py:27
  21.8 36.7 %all-to-all-start = ((bf16[8,80,2048]{2,1,0:T(8,128)(2,1)}), bf16[8,80,2048]{2,1,0:T(8,128)(2,1)}, u32[]{:S(2)}, u32[]{:S(2)}) async-start(bf16[8,80,2048]{2,1,0:T(8,128)(2,1)} %fusion), calls=%async_computation | async-start | bytes 5242880 | tf_op jit(solution)/shard_map/all_to_all | solution.py:26
  26.2 188.8 %all-gather.3.cloned.1.call-start = ((), (), s32[]{:S(2)}) async-start(), calls=%async_computation.2 | async-start | bytes 10485760 | tf_op jit(solution)/shard_map/all_gather | solution.py:36
Sparse Core Ops, SparseCore 0:
  66.0 149.0 all-gather.2
where the time goes:
time: 236 us
  waiting for transfers between devices  175 us (74%)
  matrix products  13.9 us (6%)
  between operations  13.4 us (6%)
  local copies, waits for them, and re-layouts  12.8 us (5%)
  other arithmetic  11.1 us (5%)
  starting transfers between devices  9.6 us (4%)
    all_gather x1, waiting for transfers between devices, shards(): lax.all_gather(compact, 'hidden', axis=0, tiled=True)  149 us
    all_to_all x1, waiting for transfers between devices, shards(): lax.all_to_all(scaled, 'expert', split_axis=0, concat_axis=0, tiled=True)  25.8 us
    dot_general x1, matrix products, shards(): jnp.einsum('rd,fd->rf', lax.all_gather(compact, 'hidden', axis=0, tiled=T...  13.9 us
    gather x1, local copies, waits for them, and re-layouts, pick_live(): return flat_rows[flat_index]  7.3 us
    gather x3, other arithmetic, pick_live(): flat_index = source * slot_width + row_number - first_slot[source]  5.21 us
    all_to_all x1, starting transfers between devices, shards(): lax.all_to_all(slot_count, 'expert', split_axis=0, concat_axis=0, tiled=T...  5.17 us
  transfers between devices with their start and end apart: 3, of which 2 were waited for; matrix products, arithmetic and copies ran while one was open for 6% of the time, Pallas kernels for 0%

commit v1 on v0

v1 whole, which is shorter than its diff:
```python
import functools

import jax
import jax.numpy as jnp
import numpy as np
from jax import lax
from jax.experimental import pallas as pl
from jax.experimental.pallas import tpu as pltpu
from jax.sharding import PartitionSpec as P

CF = 2
TILE = 256
MESH = pl.DeviceIdType.MESH


def nt_dot(a, b):
    return lax.dot_general(a, b, (((1,), (1,)), ((), ())), preferred_element_type=jnp.float32)


def kernel(
    n_ex, n_hid, slots, cot, meta_in, info, w_hbm, out_hbm,
    raw, meta, cnt, cnts, send_a, send_b, got_a, got_b, routed_b, routed_a, weight, stage,
    raw_send, raw_recv, meta_send, meta_recv, cnt_send, cnt_recv,
    a_send, a_recv, b_send, b_recv, rb_send, rb_recv, w_sem, out_sem,
):
    ex, hid = lax.axis_index("expert"), lax.axis_index("hidden")
    tokens = cot.shape[0]
    wide = raw.shape[2]
    narrow = send_b.shape[1]
    group = routed_b.shape[1]
    lanes = meta.shape[2]
    peers_rows = (n_ex - 1) * slots

    def rows_of(i):
        return pl.ds(pl.multiple_of(i * slots, 16), slots)

    barrier = pltpu.get_barrier_semaphore()

    def greet_plane(i, carry):
        pl.semaphore_signal(barrier, inc=1, device_id={"expert": lax.rem(ex + i, n_ex)}, device_id_type=MESH)
        return carry

    def greet_line(i, carry):
        pl.semaphore_signal(barrier, inc=1, device_id={"hidden": lax.rem(hid + i, n_hid)}, device_id_type=MESH)
        return carry

    lax.fori_loop(1, n_ex, greet_plane, 0)
    lax.fori_loop(1, n_hid, greet_line, 0)
    pl.semaphore_wait(barrier, n_ex + n_hid - 2)

    weight_copy = pltpu.make_async_copy(w_hbm.at[0], weight, w_sem)

    def meta_copy(i):
        return pltpu.make_async_remote_copy(
            src_ref=meta_in, dst_ref=meta.at[hid], send_sem=meta_send.at[i], recv_sem=meta_recv.at[hid],
            device_id={"hidden": lax.rem(hid + i, n_hid)}, device_id_type=MESH,
        )

    def line_copy(src, dst, send, recv, way, shard):
        return pltpu.make_async_remote_copy(
            src_ref=src, dst_ref=dst, send_sem=send.at[way, shard], recv_sem=recv.at[shard],
            device_id={"hidden": hid + 1 - 2 * way}, device_id_type=MESH,
        )

    def has_next(way):
        after = hid + 1 - 2 * way
        return (after >= 0) & (after < n_hid)

    def both_ways(body):
        def step(way, carry):
            body(way)
            return carry

        lax.fori_loop(0, 2, step, 0)

    def start_raw(way):
        @pl.when(has_next(way))
        def _():
            line_copy(cot.at[:, pl.ds(0, wide)], raw.at[hid], raw_send, raw_recv, way, hid).start()

    for i in range(1, n_hid):
        meta_copy(i).start()
    both_ways(start_raw)
    meta[hid] = meta_in[...]

    lane = lax.broadcasted_iota(jnp.int32, (slots, lanes), 1)
    token_iota = lax.broadcasted_iota(jnp.int32, (slots, tokens), 1).astype(jnp.float32)

    def choice(shard, expert):
        held = meta[shard]
        token = jnp.sum(jnp.where(lane == expert, held, 0.0), axis=1, keepdims=True)
        gate = jnp.sum(jnp.where(lane == expert + n_ex, held, 0.0), axis=1, keepdims=True)
        return jnp.where(token == token_iota, 1.0, 0.0).astype(jnp.bfloat16), gate

    def scaled(picked, gate, rows):
        return (gate * jnp.dot(picked, rows, preferred_element_type=jnp.float32)).astype(jnp.bfloat16)

    def a_copy(shard, expert):
        return pltpu.make_async_remote_copy(
            src_ref=send_a.at[shard, rows_of(expert)], dst_ref=got_a.at[shard, rows_of(ex)],
            send_sem=a_send.at[shard], recv_sem=a_recv.at[shard],
            device_id={"expert": expert}, device_id_type=MESH,
        )

    def b_copy(expert):
        return pltpu.make_async_remote_copy(
            src_ref=send_b.at[rows_of(expert)], dst_ref=got_b.at[rows_of(ex)],
            send_sem=b_send, recv_sem=b_recv, device_id={"expert": expert}, device_id_type=MESH,
        )

    def send_narrow(i, carry):
        expert = lax.rem(ex + i, n_ex)
        picked, gate = choice(hid, expert)
        send_b[rows_of(expert), :] = scaled(picked, gate, cot[:, wide:])
        b_copy(expert).start()
        return carry

    lax.fori_loop(1, n_ex, send_narrow, 0)
    picked, gate = choice(hid, ex)
    got_b[rows_of(ex), :] = scaled(picked, gate, cot[:, wide:])

    def send_wide(shard, rows):
        def one(i, carry):
            expert = lax.rem(ex + i, n_ex)
            picked, gate = choice(shard, expert)
            send_a[shard, rows_of(expert), :] = scaled(picked, gate, rows())
            a_copy(shard, expert).start()
            return carry

        lax.fori_loop(1, n_ex, one, 0)
        picked, gate = choice(shard, ex)
        got_a[shard, rows_of(ex), :] = scaled(picked, gate, rows())

    send_wide(hid, lambda: cot[:, :wide])
    weight_copy.start()

    for i in range(1, n_hid):
        source = lax.rem(hid + i, n_hid)
        pltpu.make_async_copy(meta.at[source], meta.at[source], meta_recv.at[source]).wait()
    cnt[...] = jnp.zeros(cnt.shape, cnt.dtype)
    for shard in range(n_hid):
        live = jnp.where((meta[shard] >= 0.0) & (lane < n_ex), 1.0, 0.0)
        cnt[shard : shard + 1, :] = jnp.sum(live, axis=0, keepdims=True)

    def cnt_copy(i):
        return pltpu.make_async_remote_copy(
            src_ref=cnt, dst_ref=cnts.at[ex], send_sem=cnt_send, recv_sem=cnt_recv,
            device_id={"expert": lax.rem(ex + i, n_ex)}, device_id_type=MESH,
        )

    def send_cnt(i, carry):
        cnt_copy(i).start()
        return carry

    lax.fori_loop(1, n_ex, send_cnt, 0)
    cnts[ex] = cnt[...]
    pltpu.make_async_copy(cnts.at[pl.ds(0, n_ex - 1)], cnts.at[pl.ds(0, n_ex - 1)], cnt_recv).wait()

    one_lane = lax.broadcasted_iota(jnp.int32, (1, lanes), 1)

    def order(shard):
        owner, place = info[0:1, :], info[1:2, :]

        def add(source, carry):
            first, own = carry
            row = cnts[source, pl.ds(shard, 1), :]
            count = jnp.sum(jnp.where(one_lane == ex, row, 0.0), axis=1, keepdims=True)
            at = source.astype(jnp.float32)
            return first + jnp.where(owner > at, count, 0.0), own + jnp.where(owner == at, count, 0.0)

        zero = jnp.zeros(owner.shape, jnp.float32)
        first, own = lax.fori_loop(0, n_ex, add, (zero, zero))
        target = jnp.where(place < own, first + place, -1.0)
        row = lax.broadcasted_iota(jnp.int32, (group, owner.shape[1]), 0).astype(jnp.float32)
        return jnp.where(row == target, 1.0, 0.0).astype(jnp.bfloat16)

    pltpu.make_async_copy(got_b.at[pl.ds(0, peers_rows)], got_b.at[pl.ds(0, peers_rows)], b_recv).wait()
    routed_b[hid] = jnp.dot(order(hid), got_b[...], preferred_element_type=jnp.float32).astype(jnp.bfloat16)

    def start_routed(way):
        @pl.when(has_next(way))
        def _():
            line_copy(routed_b.at[hid], routed_b.at[hid], rb_send, rb_recv, way, hid).start()

    both_ways(start_routed)

    def on_line(step, body):
        def one(way):
            shard = hid - step + 2 * step * way

            @pl.when((shard >= 0) & (shard < n_hid))
            def _():
                body(way, shard)

        both_ways(one)

    def take_raw(way, shard):
        pltpu.make_async_copy(raw.at[shard], raw.at[shard], raw_recv.at[shard]).wait()

        @pl.when(has_next(way))
        def _():
            line_copy(raw.at[shard], raw.at[shard], raw_send, raw_recv, way, shard).start()

        send_wide(shard, lambda: raw[shard])

    def take_routed(way, shard):
        pltpu.make_async_copy(routed_b.at[shard], routed_b.at[shard], rb_recv.at[shard]).wait()

        @pl.when(has_next(way))
        def _():
            line_copy(routed_b.at[shard], routed_b.at[shard], rb_send, rb_recv, way, shard).start()

    def along(step, carry):
        on_line(step, take_raw)
        on_line(step, take_routed)
        return carry

    lax.fori_loop(1, n_hid, along, 0)
    weight_copy.wait()

    def out_copy(shard):
        rows = pl.ds(pl.multiple_of(shard * group, 16), group)
        return pltpu.make_async_copy(stage.at[shard], out_hbm.at[0, rows], out_sem.at[shard])

    def finish(shard):
        @pl.when(n_ex > 1)
        def _():
            part = got_a.at[shard, pl.ds(0, peers_rows)]
            pltpu.make_async_copy(part, part, a_recv.at[shard]).wait()

        put = order(shard)

        def compact(c, carry):
            columns = pl.ds(pl.multiple_of(c * TILE, TILE), TILE)
            part = jnp.dot(put, got_a[shard, :, columns], preferred_element_type=jnp.float32)
            routed_a[:, columns] = part.astype(jnp.bfloat16)
            return carry

        lax.fori_loop(0, wide // TILE, compact, 0)

        def multiply(c, carry):
            columns = pl.ds(pl.multiple_of(c * TILE, TILE), TILE)
            total = nt_dot(routed_a[...], weight[columns, :wide]) + nt_dot(routed_b[shard], weight[columns, wide:])
            stage[shard, :, columns] = total.astype(jnp.bfloat16)
            return carry

        lax.fori_loop(0, stage.shape[2] // TILE, multiply, 0)
        out_copy(shard).start()

    def finish_step(m, carry):
        step, way = (m + 1) // 2, lax.rem(m + 1, 2)
        shard = hid - step + 2 * step * way

        @pl.when((shard >= 0) & (shard < n_hid))
        def _():
            finish(shard)

        return carry

    lax.fori_loop(0, 2 * n_hid - 1, finish_step, 0)

    for shard in range(n_hid):
        out_copy(shard).wait()
        part = send_a.at[shard, pl.ds(0, peers_rows)]
        pltpu.make_async_copy(part, part, a_send.at[shard]).wait()
        for way in range(2):
            sent = has_next(way) & ((shard <= hid) if way == 0 else (shard >= hid))

            @pl.when(sent)
            def _():
                line_copy(raw.at[shard], raw.at[shard], raw_send, raw_recv, way, shard).wait_send()
                line_copy(routed_b.at[shard], routed_b.at[shard], rb_send, rb_recv, way, shard).wait_send()

    part = send_b.at[pl.ds(0, peers_rows)]
    pltpu.make_async_copy(part, part, b_send).wait()
    pltpu.make_async_copy(cnts.at[pl.ds(0, n_ex - 1)], cnts.at[pl.ds(0, n_ex - 1)], cnt_send).wait()
    for i in range(1, n_hid):
        meta_copy(i).wait_send()


def shards(n_ex, n_hid, cotangent, slot_token, slot_gate, w_down):
    tokens, features = cotangent.shape
    hidden = w_down.shape[1]
    slots = -(-slot_token.shape[2] // 16) * 16
    lanes = -(-2 * n_ex // 128) * 128
    wide = features * 3 // 4 // TILE * TILE
    narrow = features - wide
    group = CF * tokens
    spare = ((0, slots - slot_token.shape[2]), (0, 0))
    token = jnp.pad(slot_token[0].T.astype(jnp.float32), spare, constant_values=-1.0)
    gate = jnp.pad(slot_gate[0].T, spare)
    meta = jnp.pad(jnp.concatenate([token, gate], axis=1), ((0, 0), (0, lanes - 2 * n_ex)))
    place = np.arange(n_ex * slots)
    info = np.zeros((8, n_ex * slots), np.float32)
    info[0], info[1] = place // slots, place % slots
    dma = pltpu.SemaphoreType.DMA
    bf16, f32 = jnp.bfloat16, jnp.float32
    vmem = pl.BlockSpec(memory_space=pltpu.VMEM)
    return pl.pallas_call(
        functools.partial(kernel, n_ex, n_hid, slots),
        out_shape=jax.ShapeDtypeStruct((1, n_hid * group, hidden), bf16),
        in_specs=[vmem, vmem, vmem, pl.BlockSpec(memory_space=pl.ANY)],
        out_specs=pl.BlockSpec(memory_space=pl.ANY),
        scratch_shapes=[
            pltpu.VMEM((n_hid, tokens, wide), bf16),
            pltpu.VMEM((n_hid, slots, lanes), f32),
            pltpu.VMEM((-(-n_hid // 8) * 8, lanes), f32),
            pltpu.VMEM((n_ex, -(-n_hid // 8) * 8, lanes), f32),
            pltpu.VMEM((n_hid, n_ex * slots, wide), bf16),
            pltpu.VMEM((n_ex * slots, narrow), bf16),
            pltpu.VMEM((n_hid, n_ex * slots, wide), bf16),
            pltpu.VMEM((n_ex * slots, narrow), bf16),
            pltpu.VMEM((n_hid, group, narrow), bf16),
            pltpu.VMEM((group, wide), bf16),
            pltpu.VMEM((hidden, features), bf16),
            pltpu.VMEM((n_hid, group, hidden), bf16),
            dma((2, n_hid)), dma((n_hid,)), dma((n_hid,)), dma((n_hid,)), dma, dma,
            dma((n_hid,)), dma((n_hid,)), dma, dma, dma((2, n_hid)), dma((n_hid,)), dma, dma((n_hid,)),
        ],
        compiler_params=pltpu.CompilerParams(
            collective_id=0, has_side_effects=True, vmem_limit_bytes=60 * 1024 * 1024
        ),
        cost_estimate=pl.CostEstimate(
            flops=2 * n_hid * group * hidden * features, bytes_accessed=2 * hidden * features * 3, transcendentals=0
        ),
        name="route_and_multiply",
    )(cotangent, meta, jnp.asarray(info), w_down)


def solution(mesh):
    n_ex, n_hid = mesh.shape["expert"], mesh.shape["hidden"]
    in_specs = (
        P(("expert", "hidden"), None),
        P(("expert", "hidden"), None, None),
        P(("expert", "hidden"), None, None),
        P("expert", "hidden", None),
    )
    out_specs = P("expert", None, "hidden")
    return jax.shard_map(
        functools.partial(shards, n_ex, n_hid), mesh=mesh, in_specs=in_specs, out_specs=out_specs, check_vma=False
    )
```

time: 236 us -> 140 us (0.59)
  waiting for transfers between devices: 175 us -> 0 us
  Pallas kernels: 0 us -> 133 us
  matrix products: 13.9 us -> 0 us
  between operations: 13.4 us -> 0.01 us
  other arithmetic: 11.1 us -> 1.38 us
  starting transfers between devices: 9.6 us -> 0 us
  local copies, waits for them, and re-layouts: 12.8 us -> 5.36 us
    all_gather x1 -> x0, waiting for transfers between devices: 149 us -> none  [shards(): lax.all_gather(compact, 'hidden', axis=0, tiled=True)]
    pallas_call x0 -> x1, Pallas kernels: none -> 133 us  [shards(): pl.pallas_call(functools.partial(kernel, n_ex, n_hid, slots), out_shape=j...]
    all_to_all x2 -> x0, waiting for transfers between devices: 25.8 us -> none  [the longest x1 25.8 us: shards(): lax.all_to_all(scaled, 'expert', split_axis=0, concat_axis=0, tiled=True)]
    dot_general x1 -> x0, matrix products: 13.9 us -> none  [shards(): jnp.einsum('rd,fd->rf', lax.all_gather(compact, 'hidden', axis=0, tiled=T...]
    gather x3 -> x0, local copies, waits for them, and re-layouts: 12.1 us -> none  [the longest x1 7.3 us: pick_live(): return flat_rows[flat_index]]
    all_to_all x2 -> x0, starting transfers between devices: 9.55 us -> none  [the longest x1 5.17 us: shards(): lax.all_to_all(slot_count, 'expert', split_axis=0, concat_axis=0, tiled=T...]
    gather x5 -> x0, other arithmetic: 5.23 us -> none  [the longest x3 5.21 us: pick_live(): flat_index = source * slot_width + row_number - first_slot[source]]
    unnamed x2 -> x1, local copies, waits for them, and re-layouts: 0.01 us -> 4.64 us
  transfers between devices with their start and end apart: 3 -> 0, of which waited for: 2 -> 0; matrix products, arithmetic and copies ran while one was open for 6% -> 0% of each run, Pallas kernels for 0% -> 0%
where the time goes in v1:
time: 140 us
  Pallas kernels  133 us (95%)
  local copies, waits for them, and re-layouts  5.36 us (4%)
    pallas_call x1, Pallas kernels, shards(): pl.pallas_call(functools.partial(kernel, n_ex, n_hid, slots), out_shape=j...  133 us
    unnamed x1, local copies, waits for them, and re-layouts  4.64 us

profile of v1, /device:TPU:0, one launch (start us, length us, event | category | flops | bytes accessed | tf_op | source)
XLA Modules:
  0.0 140.0 jit_solution(12364964533745911450)
XLA Ops:
  0.0 0.7 convert_bitcast_fusion
  0.7 0.7 pad_maximum_fusion
  1.4 0.1 copy.8
  1.5 0.6 pad.4.meta_in
  2.1 133.2 %route_and_multiply.1 = bf16[1,2048,1024]{2,1,0:T(8,128)(2,1)} custom-call(bf16[256,2048]{1,0:T(8,128)(2,1)} %cot.1, f32[80,128]{1,0:T(8,128)} %pad.4.meta_in, f32[8,640]{1,0:T(8,128)} %constant.6.clone.info, bf16[1,1024,2048]{2,1,0:T(8,128)(2,1)} %w_hbm.1), custom_call_target="tpu_custom_call" | custom-call | flops 8589934592 | bytes 12582912 | tf_op jit(solution)/shard_map/route_and_multiply/pallas_call | solution.py:299
  135.3 4.6 %copy.10 = bf16[1,2048,1024]{2,1,0:T(8,128)(2,1)} copy(bf16[1,2048,1024]{2,1,0:T(8,128)(2,1)} %route_and_multiply.1) | data formatting | bytes 8388608

commit v2 on v1

--- a/solution.py
+++ b/solution.py
@@ -18,10 +18,10 @@
 
 
 def kernel(
-    n_ex, n_hid, slots, cot, meta_in, info, w_hbm, out_hbm,
-    raw, meta, cnt, cnts, send_a, send_b, got_a, got_b, routed_b, routed_a, weight, stage,
+    n_ex, n_hid, slots, cot, token_in, gate_in, info, w_hbm, stage,
+    raw, table, meta, cnt, cnts, send_a, send_b, got_a, got_b, routed_b, routed_a, weight,
     raw_send, raw_recv, meta_send, meta_recv, cnt_send, cnt_recv,
-    a_send, a_recv, b_send, b_recv, rb_send, rb_recv, w_sem, out_sem,
+    a_send, a_recv, b_send, b_recv, rb_send, rb_recv, w_sem,
 ):
     ex, hid = lax.axis_index("expert"), lax.axis_index("hidden")
     tokens = cot.shape[0]
@@ -52,7 +52,7 @@
 
     def meta_copy(i):
         return pltpu.make_async_remote_copy(
-            src_ref=meta_in, dst_ref=meta.at[hid], send_sem=meta_send.at[i], recv_sem=meta_recv.at[hid],
+            src_ref=meta.at[hid], dst_ref=meta.at[hid], send_sem=meta_send.at[i], recv_sem=meta_recv.at[hid],
             device_id={"hidden": lax.rem(hid + i, n_hid)}, device_id_type=MESH,
         )
 
@@ -78,10 +78,14 @@
         def _():
             line_copy(cot.at[:, pl.ds(0, wide)], raw.at[hid], raw_send, raw_recv, way, hid).start()
 
+    both_ways(start_raw)
+    live_slots = token_in.shape[2]
+    table[...] = jnp.where(lax.broadcasted_iota(jnp.int32, table.shape, 0) < n_ex, -1.0, 0.0)
+    table[0:n_ex, 0:live_slots] = token_in[0].astype(jnp.float32)
+    table[n_ex : 2 * n_ex, 0:live_slots] = gate_in[0]
+    meta[hid] = table[...].T[0:slots, :]
     for i in range(1, n_hid):
         meta_copy(i).start()
-    both_ways(start_raw)
-    meta[hid] = meta_in[...]
 
     lane = lax.broadcasted_iota(jnp.int32, (slots, lanes), 1)
     token_iota = lax.broadcasted_iota(jnp.int32, (slots, tokens), 1).astype(jnp.float32)
@@ -182,8 +186,6 @@
         def _():
             line_copy(routed_b.at[hid], routed_b.at[hid], rb_send, rb_recv, way, hid).start()
 
-    both_ways(start_routed)
-
     def on_line(step, body):
         def one(way):
             shard = hid - step + 2 * step * way
@@ -212,15 +214,26 @@
 
     def along(step, carry):
         on_line(step, take_raw)
+        last_raw(step)
+        return carry
+
+    def last_raw(step):
+        def one(way):
+            @pl.when(step == hid + way * (n_hid - 1 - 2 * hid))
+            def _():
+                start_routed(way)
+
+        both_ways(one)
+
+    last_raw(0)
+    lax.fori_loop(1, n_hid, along, 0)
+
+    def along_routed(step, carry):
         on_line(step, take_routed)
         return carry
 
-    lax.fori_loop(1, n_hid, along, 0)
+    lax.fori_loop(1, n_hid, along_routed, 0)
     weight_copy.wait()
-
-    def out_copy(shard):
-        rows = pl.ds(pl.multiple_of(shard * group, 16), group)
-        return pltpu.make_async_copy(stage.at[shard], out_hbm.at[0, rows], out_sem.at[shard])
 
     def finish(shard):
         @pl.when(n_ex > 1)
@@ -241,11 +254,11 @@
         def multiply(c, carry):
             columns = pl.ds(pl.multiple_of(c * TILE, TILE), TILE)
             total = nt_dot(routed_a[...], weight[columns, :wide]) + nt_dot(routed_b[shard], weight[columns, wide:])
-            stage[shard, :, columns] = total.astype(jnp.bfloat16)
+            stage[0, rows, columns] = total.astype(jnp.bfloat16)
             return carry
 
+        rows = pl.ds(pl.multiple_of(shard * group, 16), group)
         lax.fori_loop(0, stage.shape[2] // TILE, multiply, 0)
-        out_copy(shard).start()
 
     def finish_step(m, carry):
         step, way = (m + 1) // 2, lax.rem(m + 1, 2)
@@ -260,7 +273,6 @@
     lax.fori_loop(0, 2 * n_hid - 1, finish_step, 0)
 
     for shard in range(n_hid):
-        out_copy(shard).wait()
         part = send_a.at[shard, pl.ds(0, peers_rows)]
         pltpu.make_async_copy(part, part, a_send.at[shard]).wait()
         for way in range(2):
@@ -286,10 +298,6 @@
     wide = features * 3 // 4 // TILE * TILE
     narrow = features - wide
     group = CF * tokens
-    spare = ((0, slots - slot_token.shape[2]), (0, 0))
-    token = jnp.pad(slot_token[0].T.astype(jnp.float32), spare, constant_values=-1.0)
-    gate = jnp.pad(slot_gate[0].T, spare)
-    meta = jnp.pad(jnp.concatenate([token, gate], axis=1), ((0, 0), (0, lanes - 2 * n_ex)))
     place = np.arange(n_ex * slots)
     info = np.zeros((8, n_ex * slots), np.float32)
     info[0], info[1] = place // slots, place % slots
@@ -298,11 +306,12 @@
     vmem = pl.BlockSpec(memory_space=pltpu.VMEM)
     return pl.pallas_call(
         functools.partial(kernel, n_ex, n_hid, slots),
-        out_shape=jax.ShapeDtypeStruct((1, n_hid * group, hidden), bf16),
-        in_specs=[vmem, vmem, vmem, pl.BlockSpec(memory_space=pl.ANY)],
-        out_specs=pl.BlockSpec(memory_space=pl.ANY),
+        out_shape=pltpu.VMEM((1, n_hid * group, hidden), bf16),
+        in_specs=[vmem, vmem, vmem, vmem, pl.BlockSpec(memory_space=pl.ANY)],
+        out_specs=vmem,
         scratch_shapes=[
             pltpu.VMEM((n_hid, tokens, wide), bf16),
+            pltpu.VMEM((lanes, 128), f32),
             pltpu.VMEM((n_hid, slots, lanes), f32),
             pltpu.VMEM((-(-n_hid // 8) * 8, lanes), f32),
             pltpu.VMEM((n_ex, -(-n_hid // 8) * 8, lanes), f32),
@@ -313,18 +322,17 @@
             pltpu.VMEM((n_hid, group, narrow), bf16),
             pltpu.VMEM((group, wide), bf16),
             pltpu.VMEM((hidden, features), bf16),
-            pltpu.VMEM((n_hid, group, hidden), bf16),
             dma((2, n_hid)), dma((n_hid,)), dma((n_hid,)), dma((n_hid,)), dma, dma,
-            dma((n_hid,)), dma((n_hid,)), dma, dma, dma((2, n_hid)), dma((n_hid,)), dma, dma((n_hid,)),
+            dma((n_hid,)), dma((n_hid,)), dma, dma, dma((2, n_hid)), dma((n_hid,)), dma,
         ],
         compiler_params=pltpu.CompilerParams(
-            collective_id=0, has_side_effects=True, vmem_limit_bytes=60 * 1024 * 1024
+            collective_id=0, has_side_effects=True, vmem_limit_bytes=48 * 1024 * 1024
         ),
         cost_estimate=pl.CostEstimate(
             flops=2 * n_hid * group * hidden * features, bytes_accessed=2 * hidden * features * 3, transcendentals=0
         ),
         name="route_and_multiply",
-    )(cotangent, meta, jnp.asarray(info), w_down)
+    )(cotangent, slot_token, slot_gate, jnp.asarray(info), w_down)
 
 
 def solution(mesh):

time: 140 us -> 140 us (level)
  Pallas kernels: 133 us -> 135 us
    unnamed x1 -> x9, local copies, waits for them, and re-layouts: 4.64 us -> 5.34 us
where the time goes in v2:
time: 140 us
  Pallas kernels  135 us (96%)
  local copies, waits for them, and re-layouts  5.34 us (4%)
    pallas_call x1, Pallas kernels, shards(): pl.pallas_call(functools.partial(kernel, n_ex, n_hid, slots), out_shape=p...  135 us
    unnamed x9, local copies, waits for them, and re-layouts  5.34 us

profile of v2, /device:TPU:0, one launch (start us, length us, event | category | flops | bytes accessed | tf_op | source)
XLA Modules:
  0.0 139.9 jit_solution(10502214943226082150)
XLA Ops:
  0.0 0.0 copy-start
  0.0 1.2 copy-done
  1.2 0.0 copy-start.1
  1.2 0.7 copy-done.1
  1.9 0.0 copy-start.2
  1.9 0.7 copy-done.2
  2.6 0.0 copy-start.3
  2.6 0.7 copy-done.3
  3.3 134.6 %route_and_multiply.1 = bf16[1,2048,1024]{2,1,0:T(8,128)(2,1)S(1)} custom-call(bf16[256,2048]{1,0:T(8,128)(2,1)S(1)} %copy-done, s32[1,8,80]{2,1,0:T(8,128)S(1)} %copy-done.1, f32[1,8,80]{2,1,0:T(8,128)S(1)} %copy-done.2, f32[8,640]{1,0:T(8,128)S(1)} %copy-done.3, bf16[1,1024,2048]{2,1,0:T(8,128)(2,1)} %w_hbm.1), custom_call_target="tpu_custom_call" | custom-call | flops 8589934592 | bytes 12582912 | tf_op jit(solution)/shard_map/route_and_multiply/pallas_call | solution.py:307
  137.9 2.0 %copy.7 = bf16[1,2048,1024]{2,1,0:T(8,128)(2,1)} copy(bf16[1,2048,1024]{2,1,0:T(8,128)(2,1)S(1)} %route_and_multiply.1) | data formatting | bytes 8388608
Async XLA Ops:
  0.0 1.2 copy-start
  1.2 0.7 copy-start.1
  1.9 0.7 copy-start.2
  2.6 0.7 copy-start.3

commit v3 on v2

--- a/solution.py
+++ b/solution.py
@@ -2,7 +2,6 @@
 
 import jax
 import jax.numpy as jnp
-import numpy as np
 from jax import lax
 from jax.experimental import pallas as pl
 from jax.experimental.pallas import tpu as pltpu
@@ -13,15 +12,12 @@
 MESH = pl.DeviceIdType.MESH
 
 
-def nt_dot(a, b):
-    return lax.dot_general(a, b, (((1,), (1,)), ((), ())), preferred_element_type=jnp.float32)
-
-
 def kernel(
-    n_ex, n_hid, slots, cot, token_in, gate_in, info, w_hbm, stage,
+    n_ex, n_hid, slots, cot_hbm, token_hbm, gate_hbm, w_hbm, stage,
+    cot, token_in, gate_in, pick, gates, put, weight_t,
     raw, table, meta, cnt, cnts, send_a, send_b, got_a, got_b, routed_b, routed_a, weight,
     raw_send, raw_recv, meta_send, meta_recv, cnt_send, cnt_recv,
-    a_send, a_recv, b_send, b_recv, rb_send, rb_recv, w_sem,
+    a_send, a_recv, b_send, b_recv, rb_send, rb_recv, load_sem,
 ):
     ex, hid = lax.axis_index("expert"), lax.axis_index("hidden")
     tokens = cot.shape[0]
@@ -34,6 +30,15 @@
     def rows_of(i):
         return pl.ds(pl.multiple_of(i * slots, 16), slots)
 
+    loads = [
+        pltpu.make_async_copy(source, target, load_sem.at[i])
+        for i, (source, target) in enumerate(
+            [(token_hbm, token_in), (gate_hbm, gate_in), (cot_hbm, cot), (w_hbm.at[0], weight)]
+        )
+    ]
+    for load in loads:
+        load.start()
+
     barrier = pltpu.get_barrier_semaphore()
 
     def greet_plane(i, carry):
@@ -48,8 +53,6 @@
     lax.fori_loop(1, n_hid, greet_line, 0)
     pl.semaphore_wait(barrier, n_ex + n_hid - 2)
 
-    weight_copy = pltpu.make_async_copy(w_hbm.at[0], weight, w_sem)
-
     def meta_copy(i):
         return pltpu.make_async_remote_copy(
             src_ref=meta.at[hid], dst_ref=meta.at[hid], send_sem=meta_send.at[i], recv_sem=meta_recv.at[hid],
@@ -76,9 +79,11 @@
     def start_raw(way):
         @pl.when(has_next(way))
         def _():
-            line_copy(cot.at[:, pl.ds(0, wide)], raw.at[hid], raw_send, raw_recv, way, hid).start()
+            line_copy(cot_hbm.at[:, pl.ds(0, wide)], raw.at[hid], raw_send, raw_recv, way, hid).start()
 
     both_ways(start_raw)
+    loads[0].wait()
+    loads[1].wait()
     live_slots = token_in.shape[2]
     table[...] = jnp.where(lax.broadcasted_iota(jnp.int32, table.shape, 0) < n_ex, -1.0, 0.0)
     table[0:n_ex, 0:live_slots] = token_in[0].astype(jnp.float32)
@@ -90,14 +95,28 @@
     lane = lax.broadcasted_iota(jnp.int32, (slots, lanes), 1)
     token_iota = lax.broadcasted_iota(jnp.int32, (slots, tokens), 1).astype(jnp.float32)
 
-    def choice(shard, expert):
+    def choose(shard):
         held = meta[shard]
-        token = jnp.sum(jnp.where(lane == expert, held, 0.0), axis=1, keepdims=True)
-        gate = jnp.sum(jnp.where(lane == expert + n_ex, held, 0.0), axis=1, keepdims=True)
-        return jnp.where(token == token_iota, 1.0, 0.0).astype(jnp.bfloat16), gate
-
-    def scaled(picked, gate, rows):
-        return (gate * jnp.dot(picked, rows, preferred_element_type=jnp.float32)).astype(jnp.bfloat16)
+
+        def one(expert, carry):
+            token = jnp.sum(jnp.where(lane == expert, held, 0.0), axis=1, keepdims=True)
+            gate = jnp.sum(jnp.where(lane == expert + n_ex, held, 0.0), axis=1, keepdims=True)
+            pick[rows_of(expert), :] = jnp.where(token == token_iota, 1.0, 0.0).astype(jnp.bfloat16)
+            gates[rows_of(expert), :] = jnp.broadcast_to(gate, (slots, TILE))
+            return carry
+
+        lax.fori_loop(0, n_ex, one, 0)
+
+    def scale(rows, store, columns):
+        def one(c, carry):
+            part = jnp.dot(pick[...], rows(c), preferred_element_type=jnp.float32)
+            store(c, (gates[...] * part).astype(jnp.bfloat16))
+            return carry
+
+        lax.fori_loop(0, columns // TILE, one, 0)
+
+    def tile(c, base=0):
+        return pl.ds(pl.multiple_of(base + c * TILE, TILE), TILE)
 
     def a_copy(shard, expert):
         return pltpu.make_async_remote_copy(
@@ -112,31 +131,32 @@
             send_sem=b_send, recv_sem=b_recv, device_id={"expert": expert}, device_id_type=MESH,
         )
 
-    def send_narrow(i, carry):
-        expert = lax.rem(ex + i, n_ex)
-        picked, gate = choice(hid, expert)
-        send_b[rows_of(expert), :] = scaled(picked, gate, cot[:, wide:])
-        b_copy(expert).start()
-        return carry
-
-    lax.fori_loop(1, n_ex, send_narrow, 0)
-    picked, gate = choice(hid, ex)
-    got_b[rows_of(ex), :] = scaled(picked, gate, cot[:, wide:])
+    def store_narrow(c, part):
+        send_b[:, tile(c)] = part
+
+    def start_narrow(i, carry):
+        b_copy(lax.rem(ex + i, n_ex)).start()
+        return carry
+
+    choose(hid)
+    loads[2].wait()
+    scale(lambda c: cot[:, tile(c, wide)], store_narrow, narrow)
+    lax.fori_loop(1, n_ex, start_narrow, 0)
+    got_b[rows_of(ex), :] = send_b[rows_of(ex), :]
 
     def send_wide(shard, rows):
-        def one(i, carry):
-            expert = lax.rem(ex + i, n_ex)
-            picked, gate = choice(shard, expert)
-            send_a[shard, rows_of(expert), :] = scaled(picked, gate, rows())
-            a_copy(shard, expert).start()
-            return carry
-
-        lax.fori_loop(1, n_ex, one, 0)
-        picked, gate = choice(shard, ex)
-        got_a[shard, rows_of(ex), :] = scaled(picked, gate, rows())
-
-    send_wide(hid, lambda: cot[:, :wide])
-    weight_copy.start()
+        def store_wide(c, part):
+            send_a[shard, :, tile(c)] = part
+
+        def start_wide(i, carry):
+            a_copy(shard, lax.rem(ex + i, n_ex)).start()
+            return carry
+
+        scale(rows, store_wide, wide)
+        lax.fori_loop(1, n_ex, start_wide, 0)
+        got_a[shard, rows_of(ex), :] = send_a[shard, rows_of(ex), :]
+
+    send_wide(hid, lambda c: cot[:, tile(c)])
 
     for i in range(1, n_hid):
         source = lax.rem(hid + i, n_hid)
@@ -163,7 +183,9 @@
     one_lane = lax.broadcasted_iota(jnp.int32, (1, lanes), 1)
 
     def order(shard):
-        owner, place = info[0:1, :], info[1:2, :]
+        number = lax.broadcasted_iota(jnp.int32, (1, n_ex * slots), 1).astype(jnp.float32)
+        owner = jnp.floor((number + 0.5) / slots)
+        place = number - owner * slots
 
         def add(source, carry):
             first, own = carry
@@ -176,10 +198,12 @@
         first, own = lax.fori_loop(0, n_ex, add, (zero, zero))
         target = jnp.where(place < own, first + place, -1.0)
         row = lax.broadcasted_iota(jnp.int32, (group, owner.shape[1]), 0).astype(jnp.float32)
-        return jnp.where(row == target, 1.0, 0.0).astype(jnp.bfloat16)
+        put[shard] = jnp.where(row == target, 1.0, 0.0).astype(jnp.bfloat16)
+
+    order(hid)
 
     pltpu.make_async_copy(got_b.at[pl.ds(0, peers_rows)], got_b.at[pl.ds(0, peers_rows)], b_recv).wait()
-    routed_b[hid] = jnp.dot(order(hid), got_b[...], preferred_element_type=jnp.float32).astype(jnp.bfloat16)
+    routed_b[hid] = jnp.dot(put[hid], got_b[...], preferred_element_type=jnp.float32).astype(jnp.bfloat16)
 
     def start_routed(way):
         @pl.when(has_next(way))
@@ -203,7 +227,8 @@
         def _():
             line_copy(raw.at[shard], raw.at[shard], raw_send, raw_recv, way, shard).start()
 
-        send_wide(shard, lambda: raw[shard])
+        choose(shard)
+        send_wide(shard, lambda c: raw[shard, :, tile(c)])
 
     def take_routed(way, shard):
         pltpu.make_async_copy(routed_b.at[shard], routed_b.at[shard], rb_recv.at[shard]).wait()
@@ -226,14 +251,20 @@
         both_ways(one)
 
     last_raw(0)
+
+    def order_other(i, carry):
+        order(lax.rem(hid + i, n_hid))
+        return carry
+
+    lax.fori_loop(1, n_hid, order_other, 0)
+    loads[3].wait()
+
+    def turn(c, carry):
+        weight_t[:, tile(c)] = weight[tile(c), :].T
+        return carry
+
+    lax.fori_loop(0, weight.shape[0] // TILE, turn, 0)
     lax.fori_loop(1, n_hid, along, 0)
-
-    def along_routed(step, carry):
-        on_line(step, take_routed)
-        return carry
-
-    lax.fori_loop(1, n_hid, along_routed, 0)
-    weight_copy.wait()
 
     def finish(shard):
         @pl.when(n_ex > 1)
@@ -241,11 +272,9 @@
             part = got_a.at[shard, pl.ds(0, peers_rows)]
             pltpu.make_async_copy(part, part, a_recv.at[shard]).wait()
 
-        put = order(shard)
-
         def compact(c, carry):
             columns = pl.ds(pl.multiple_of(c * TILE, TILE), TILE)
-            part = jnp.dot(put, got_a[shard, :, columns], preferred_element_type=jnp.float32)
+            part = jnp.dot(put[shard], got_a[shard, :, columns], preferred_element_type=jnp.float32)
             routed_a[:, columns] = part.astype(jnp.bfloat16)
             return carry
 
@@ -253,24 +282,32 @@
 
         def multiply(c, carry):
             columns = pl.ds(pl.multiple_of(c * TILE, TILE), TILE)
-            total = nt_dot(routed_a[...], weight[columns, :wide]) + nt_dot(routed_b[shard], weight[columns, wide:])
+            total = jnp.dot(routed_a[...], weight_t[:wide, columns], preferred_element_type=jnp.float32)
+            total += jnp.dot(routed_b[shard], weight_t[wide:, columns], preferred_element_type=jnp.float32)
             stage[0, rows, columns] = total.astype(jnp.bfloat16)
             return carry
 
         rows = pl.ds(pl.multiple_of(shard * group, 16), group)
         lax.fori_loop(0, stage.shape[2] // TILE, multiply, 0)
 
-    def finish_step(m, carry):
-        step, way = (m + 1) // 2, lax.rem(m + 1, 2)
-        shard = hid - step + 2 * step * way
-
-        @pl.when((shard >= 0) & (shard < n_hid))
-        def _():
-            finish(shard)
-
-        return carry
-
-    lax.fori_loop(0, 2 * n_hid - 1, finish_step, 0)
+    def along_routed(step, carry):
+        @pl.when(step > 0)
+        def _():
+            on_line(step, take_routed)
+
+        def one(way, inner):
+            shard = hid - step + 2 * step * way
+
+            @pl.when((shard >= 0) & (shard < n_hid))
+            def _():
+                finish(shard)
+
+            return inner
+
+        lax.fori_loop(0, jnp.where(step > 0, 2, 1), one, 0)
+        return carry
+
+    lax.fori_loop(0, n_hid, along_routed, 0)
 
     for shard in range(n_hid):
         part = send_a.at[shard, pl.ds(0, peers_rows)]
@@ -298,18 +335,22 @@
     wide = features * 3 // 4 // TILE * TILE
     narrow = features - wide
     group = CF * tokens
-    place = np.arange(n_ex * slots)
-    info = np.zeros((8, n_ex * slots), np.float32)
-    info[0], info[1] = place // slots, place % slots
     dma = pltpu.SemaphoreType.DMA
     bf16, f32 = jnp.bfloat16, jnp.float32
-    vmem = pl.BlockSpec(memory_space=pltpu.VMEM)
+    hbm = pl.BlockSpec(memory_space=pltpu.HBM)
     return pl.pallas_call(
         functools.partial(kernel, n_ex, n_hid, slots),
         out_shape=pltpu.VMEM((1, n_hid * group, hidden), bf16),
-        in_specs=[vmem, vmem, vmem, vmem, pl.BlockSpec(memory_space=pl.ANY)],
-        out_specs=vmem,
+        in_specs=[hbm, hbm, hbm, hbm],
+        out_specs=pl.BlockSpec(memory_space=pltpu.VMEM),
         scratch_shapes=[
+            pltpu.VMEM(cotangent.shape, bf16),
+            pltpu.VMEM(slot_token.shape, jnp.int32),
+            pltpu.VMEM(slot_gate.shape, f32),
+            pltpu.VMEM((n_ex * slots, tokens), bf16),
+            pltpu.VMEM((n_ex * slots, TILE), f32),
+            pltpu.VMEM((n_hid, group, n_ex * slots), bf16),
+            pltpu.VMEM((features, hidden), bf16),
             pltpu.VMEM((n_hid, tokens, wide), bf16),
             pltpu.VMEM((lanes, 128), f32),
             pltpu.VMEM((n_hid, slots, lanes), f32),
@@ -323,16 +364,16 @@
             pltpu.VMEM((group, wide), bf16),
             pltpu.VMEM((hidden, features), bf16),
             dma((2, n_hid)), dma((n_hid,)), dma((n_hid,)), dma((n_hid,)), dma, dma,
-            dma((n_hid,)), dma((n_hid,)), dma, dma, dma((2, n_hid)), dma((n_hid,)), dma,
+            dma((n_hid,)), dma((n_hid,)), dma, dma, dma((2, n_hid)), dma((n_hid,)), dma((4,)),
         ],
         compiler_params=pltpu.CompilerParams(
-            collective_id=0, has_side_effects=True, vmem_limit_bytes=48 * 1024 * 1024
+            collective_id=0, has_side_effects=True, vmem_limit_bytes=52 * 1024 * 1024
         ),
         cost_estimate=pl.CostEstimate(
             flops=2 * n_hid * group * hidden * features, bytes_accessed=2 * hidden * features * 3, transcendentals=0
         ),
         name="route_and_multiply",
-    )(cotangent, slot_token, slot_gate, jnp.asarray(info), w_down)
+    )(cotangent, slot_token, slot_gate, w_down)
 
 
 def solution(mesh):

time: 140 us -> 123 us (0.88)
  Pallas kernels: 135 us -> 121 us
  local copies, waits for them, and re-layouts: 5.34 us -> 2.02 us
    pallas_call x1, Pallas kernels: 135 us -> 121 us  [shards(): pl.pallas_call(functools.partial(kernel, n_ex, n_hid, slots), out_shape=p...]
    unnamed x9 -> x1, local copies, waits for them, and re-layouts: 5.34 us -> 2.02 us
where the time goes in v3:
time: 123 us
  Pallas kernels  121 us (98%)
  local copies, waits for them, and re-layouts  2.02 us (2%)
    pallas_call x1, Pallas kernels, shards(): pl.pallas_call(functools.partial(kernel, n_ex, n_hid, slots), out_shape=p...  121 us

profile of v3, /device:TPU:0, one launch (start us, length us, event | category | flops | bytes accessed | tf_op | source)
XLA Modules:
  0.0 122.9 jit_solution(11014688028206231689)
XLA Ops:
  0.0 120.9 %route_and_multiply.1 = bf16[1,2048,1024]{2,1,0:T(8,128)(2,1)S(1)} custom-call(bf16[256,2048]{1,0:T(8,128)(2,1)} %cot_hbm.1, s32[1,8,80]{2,1,0:T(8,128)} %token_hbm.1, f32[1,8,80]{2,1,0:T(8,128)} %gate_hbm.1, bf16[1,1024,2048]{2,1,0:T(8,128)(2,1)} %w_hbm.1), custom_call_target="tpu_custom_call" | custom-call | flops 8589934592 | bytes 12582912 | tf_op jit(solution)/shard_map/route_and_multiply/pallas_call | solution.py:341
  120.9 2.0 %copy.6 = bf16[1,2048,1024]{2,1,0:T(8,128)(2,1)} copy(bf16[1,2048,1024]{2,1,0:T(8,128)(2,1)S(1)} %route_and_multiply.1) | data formatting | bytes 8388608

commit v4 on v3

--- a/solution.py
+++ b/solution.py
@@ -8,20 +8,22 @@
 from jax.sharding import PartitionSpec as P
 
 CF = 2
+CHUNKS = 2
 TILE = 256
 MESH = pl.DeviceIdType.MESH
 
 
 def kernel(
     n_ex, n_hid, slots, cot_hbm, token_hbm, gate_hbm, w_hbm, stage,
-    cot, token_in, gate_in, pick, gates, put, weight_t,
+    cot, token_in, gate_in, pick, gates, put, weight_t, total,
     raw, table, meta, cnt, cnts, send_a, send_b, got_a, got_b, routed_b, routed_a, weight,
     raw_send, raw_recv, meta_send, meta_recv, cnt_send, cnt_recv,
     a_send, a_recv, b_send, b_recv, rb_send, rb_recv, load_sem,
 ):
     ex, hid = lax.axis_index("expert"), lax.axis_index("hidden")
     tokens = cot.shape[0]
-    wide = raw.shape[2]
+    part = raw.shape[3]
+    wide = CHUNKS * part
     narrow = send_b.shape[1]
     group = routed_b.shape[1]
     lanes = meta.shape[2]
@@ -33,11 +35,19 @@
     loads = [
         pltpu.make_async_copy(source, target, load_sem.at[i])
         for i, (source, target) in enumerate(
-            [(token_hbm, token_in), (gate_hbm, gate_in), (cot_hbm, cot), (w_hbm.at[0], weight)]
+            [(token_hbm, token_in), (gate_hbm, gate_in), (cot_hbm, cot)]
         )
     ]
     for load in loads:
         load.start()
+
+    def weight_load(c):
+        rows = pl.ds(c * TILE, TILE)
+        return pltpu.make_async_copy(w_hbm.at[0, rows], weight.at[c % 2], load_sem.at[3 + c % 2])
+
+    w_tiles = w_hbm.shape[1] // TILE
+    for c in range(min(2, w_tiles)):
+        weight_load(c).start()
 
     barrier = pltpu.get_barrier_semaphore()
 
@@ -59,11 +69,20 @@
             device_id={"hidden": lax.rem(hid + i, n_hid)}, device_id_type=MESH,
         )
 
-    def line_copy(src, dst, send, recv, way, shard):
+    def to_next(src, dst, send, recv, way):
         return pltpu.make_async_remote_copy(
-            src_ref=src, dst_ref=dst, send_sem=send.at[way, shard], recv_sem=recv.at[shard],
+            src_ref=src, dst_ref=dst, send_sem=send, recv_sem=recv,
             device_id={"hidden": hid + 1 - 2 * way}, device_id_type=MESH,
         )
+
+    def raw_copy(way, shard, chunk, own=False):
+        held = raw.at[shard, chunk]
+        src = cot_hbm.at[:, pl.ds(chunk * part, part)] if own else held
+        return to_next(src, held, raw_send.at[way, shard, chunk], raw_recv.at[shard, chunk], way)
+
+    def routed_copy(way, shard):
+        held = routed_b.at[shard]
+        return to_next(held, held, rb_send.at[way, shard], rb_recv.at[shard], way)
 
     def has_next(way):
         after = hid + 1 - 2 * way
@@ -76,12 +95,13 @@
 
         lax.fori_loop(0, 2, step, 0)
 
-    def start_raw(way):
+    def start_raw(way, chunk):
         @pl.when(has_next(way))
         def _():
-            line_copy(cot_hbm.at[:, pl.ds(0, wide)], raw.at[hid], raw_send, raw_recv, way, hid).start()
-
-    both_ways(start_raw)
+            raw_copy(way, hid, chunk, own=True).start()
+
+    for chunk in range(CHUNKS):
+        both_ways(functools.partial(start_raw, chunk=chunk))
     loads[0].wait()
     loads[1].wait()
     live_slots = token_in.shape[2]
@@ -101,16 +121,17 @@
         def one(expert, carry):
             token = jnp.sum(jnp.where(lane == expert, held, 0.0), axis=1, keepdims=True)
             gate = jnp.sum(jnp.where(lane == expert + n_ex, held, 0.0), axis=1, keepdims=True)
-            pick[rows_of(expert), :] = jnp.where(token == token_iota, 1.0, 0.0).astype(jnp.bfloat16)
-            gates[rows_of(expert), :] = jnp.broadcast_to(gate, (slots, TILE))
+            pick[shard, rows_of(expert), :] = jnp.where(token == token_iota, 1.0, 0.0).astype(jnp.bfloat16)
+            gates[shard, rows_of(expert), :] = jnp.broadcast_to(gate, (slots, 128))
             return carry
 
         lax.fori_loop(0, n_ex, one, 0)
 
-    def scale(rows, store, columns):
+    def scale(shard, rows, store, columns):
         def one(c, carry):
-            part = jnp.dot(pick[...], rows(c), preferred_element_type=jnp.float32)
-            store(c, (gates[...] * part).astype(jnp.bfloat16))
+            rows_c = jnp.dot(pick[shard], rows(c), preferred_element_type=jnp.float32)
+            gate = jnp.concatenate([gates[shard]] * (TILE // 128), axis=1)
+            store(c, (gate * rows_c).astype(jnp.bfloat16))
             return carry
 
         lax.fori_loop(0, columns // TILE, one, 0)
@@ -118,10 +139,10 @@
     def tile(c, base=0):
         return pl.ds(pl.multiple_of(base + c * TILE, TILE), TILE)
 
-    def a_copy(shard, expert):
+    def a_copy(shard, chunk, expert):
         return pltpu.make_async_remote_copy(
-            src_ref=send_a.at[shard, rows_of(expert)], dst_ref=got_a.at[shard, rows_of(ex)],
-            send_sem=a_send.at[shard], recv_sem=a_recv.at[shard],
+            src_ref=send_a.at[shard, chunk, rows_of(expert)], dst_ref=got_a.at[shard, chunk, rows_of(ex)],
+            send_sem=a_send.at[shard, chunk], recv_sem=a_recv.at[shard, chunk],
             device_id={"expert": expert}, device_id_type=MESH,
         )
 
@@ -131,8 +152,8 @@
             send_sem=b_send, recv_sem=b_recv, device_id={"expert": expert}, device_id_type=MESH,
         )
 
-    def store_narrow(c, part):
-        send_b[:, tile(c)] = part
+    def store_narrow(c, value):
+        send_b[:, tile(c)] = value
 
     def start_narrow(i, carry):
         b_copy(lax.rem(ex + i, n_ex)).start()
@@ -140,23 +161,24 @@
 
     choose(hid)
     loads[2].wait()
-    scale(lambda c: cot[:, tile(c, wide)], store_narrow, narrow)
+    scale(hid, lambda c: cot[:, tile(c, wide)], store_narrow, narrow)
     lax.fori_loop(1, n_ex, start_narrow, 0)
     got_b[rows_of(ex), :] = send_b[rows_of(ex), :]
 
-    def send_wide(shard, rows):
-        def store_wide(c, part):
-            send_a[shard, :, tile(c)] = part
+    def send_wide(shard, chunk, rows):
+        def store_wide(c, value):
+            send_a[shard, chunk, :, tile(c)] = value
 
         def start_wide(i, carry):
-            a_copy(shard, lax.rem(ex + i, n_ex)).start()
-            return carry
-
-        scale(rows, store_wide, wide)
+            a_copy(shard, chunk, lax.rem(ex + i, n_ex)).start()
+            return carry
+
+        scale(shard, rows, store_wide, part)
         lax.fori_loop(1, n_ex, start_wide, 0)
-        got_a[shard, rows_of(ex), :] = send_a[shard, rows_of(ex), :]
-
-    send_wide(hid, lambda c: cot[:, tile(c)])
+        got_a[shard, chunk, rows_of(ex), :] = send_a[shard, chunk, rows_of(ex), :]
+
+    for chunk in range(CHUNKS):
+        send_wide(hid, chunk, lambda c: cot[:, tile(c, chunk * part)])
 
     for i in range(1, n_hid):
         source = lax.rem(hid + i, n_hid)
@@ -208,7 +230,7 @@
     def start_routed(way):
         @pl.when(has_next(way))
         def _():
-            line_copy(routed_b.at[hid], routed_b.at[hid], rb_send, rb_recv, way, hid).start()
+            routed_copy(way, hid).start()
 
     def on_line(step, body):
         def one(way):
@@ -220,25 +242,25 @@
 
         both_ways(one)
 
-    def take_raw(way, shard):
-        pltpu.make_async_copy(raw.at[shard], raw.at[shard], raw_recv.at[shard]).wait()
+    def take_raw(way, shard, chunk):
+        pltpu.make_async_copy(raw.at[shard, chunk], raw.at[shard, chunk], raw_recv.at[shard, chunk]).wait()
 
         @pl.when(has_next(way))
         def _():
-            line_copy(raw.at[shard], raw.at[shard], raw_send, raw_recv, way, shard).start()
-
-        choose(shard)
-        send_wide(shard, lambda c: raw[shard, :, tile(c)])
+            raw_copy(way, shard, chunk).start()
+
+        send_wide(shard, chunk, lambda c: raw[shard, chunk, :, tile(c)])
 
     def take_routed(way, shard):
         pltpu.make_async_copy(routed_b.at[shard], routed_b.at[shard], rb_recv.at[shard]).wait()
 
         @pl.when(has_next(way))
         def _():
-            line_copy(routed_b.at[shard], routed_b.at[shard], rb_send, rb_recv, way, shard).start()
+            routed_copy(way, shard).start()
 
     def along(step, carry):
-        on_line(step, take_raw)
+        for chunk in range(CHUNKS):
+            on_line(step, functools.partial(take_raw, chunk=chunk))
         last_raw(step)
         return carry
 
@@ -253,54 +275,85 @@
     last_raw(0)
 
     def order_other(i, carry):
-        order(lax.rem(hid + i, n_hid))
+        shard = lax.rem(hid + i, n_hid)
+        choose(shard)
+        order(shard)
         return carry
 
     lax.fori_loop(1, n_hid, order_other, 0)
-    loads[3].wait()
-
-    def turn(c, carry):
-        weight_t[:, tile(c)] = weight[tile(c), :].T
-        return carry
-
-    lax.fori_loop(0, weight.shape[0] // TILE, turn, 0)
+    for c in range(w_tiles):
+        weight_load(c).wait()
+        weight_t[:, c * TILE : (c + 1) * TILE] = weight[c % 2].T
+        if c + 2 < w_tiles:
+            weight_load(c + 2).start()
+
     lax.fori_loop(1, n_hid, along, 0)
 
-    def finish(shard):
-        @pl.when(n_ex > 1)
-        def _():
-            part = got_a.at[shard, pl.ds(0, peers_rows)]
-            pltpu.make_async_copy(part, part, a_recv.at[shard]).wait()
-
-        def compact(c, carry):
-            columns = pl.ds(pl.multiple_of(c * TILE, TILE), TILE)
-            part = jnp.dot(put[shard], got_a[shard, :, columns], preferred_element_type=jnp.float32)
-            routed_a[:, columns] = part.astype(jnp.bfloat16)
-            return carry
-
-        lax.fori_loop(0, wide // TILE, compact, 0)
-
-        def multiply(c, carry):
-            columns = pl.ds(pl.multiple_of(c * TILE, TILE), TILE)
-            total = jnp.dot(routed_a[...], weight_t[:wide, columns], preferred_element_type=jnp.float32)
-            total += jnp.dot(routed_b[shard], weight_t[wide:, columns], preferred_element_type=jnp.float32)
-            stage[0, rows, columns] = total.astype(jnp.bfloat16)
-            return carry
-
+    def product(lhs, row, columns):
+        return jnp.dot(lhs, weight_t[row : row + lhs.shape[1], columns], preferred_element_type=jnp.float32)
+
+    def compact(shard, chunk):
+        if n_ex > 1:
+            arrived = got_a.at[shard, chunk, pl.ds(0, peers_rows)]
+            pltpu.make_async_copy(arrived, arrived, a_recv.at[shard, chunk]).wait()
+
+        def one(c, carry):
+            rows = jnp.dot(put[shard], got_a[shard, chunk, :, tile(c)], preferred_element_type=jnp.float32)
+            routed_a[:, tile(c)] = rows.astype(jnp.bfloat16)
+            return carry
+
+        lax.fori_loop(0, part // TILE, one, 0)
+
+    def over_columns(body):
+        def one(c, carry):
+            body(tile(c))
+            return carry
+
+        lax.fori_loop(0, stage.shape[2] // TILE, one, 0)
+
+    def finish(way, shard, early):
+        for chunk in range(CHUNKS - 1):
+            compact(shard, chunk)
+
+            def add(columns, chunk=chunk):
+                value = product(routed_a[...], chunk * part, columns)
+                total[:, columns] = value if chunk == 0 else total[:, columns] + value
+
+            over_columns(add)
+
+        @pl.when(jnp.logical_not(early))
+        def _():
+            take_routed(way, shard)
+
+        def add_routed(columns):
+            total[:, columns] = total[:, columns] + product(routed_b[shard], wide, columns)
+
+        over_columns(add_routed)
+        compact(shard, CHUNKS - 1)
         rows = pl.ds(pl.multiple_of(shard * group, 16), group)
-        lax.fori_loop(0, stage.shape[2] // TILE, multiply, 0)
+
+        def write(columns):
+            value = total[:, columns] + product(routed_a[...], (CHUNKS - 1) * part, columns)
+            stage[0, rows, columns] = value.astype(jnp.bfloat16)
+
+        over_columns(write)
+
+    def take_to_pass(way, shard):
+        @pl.when(has_next(way))
+        def _():
+            take_routed(way, shard)
 
     def along_routed(step, carry):
         @pl.when(step > 0)
         def _():
-            on_line(step, take_routed)
+            on_line(step, take_to_pass)
 
         def one(way, inner):
             shard = hid - step + 2 * step * way
 
             @pl.when((shard >= 0) & (shard < n_hid))
             def _():
-                finish(shard)
+                finish(way, shard, (step == 0) | has_next(way))
 
             return inner
 
@@ -310,18 +363,20 @@
     lax.fori_loop(0, n_hid, along_routed, 0)
 
     for shard in range(n_hid):
-        part = send_a.at[shard, pl.ds(0, peers_rows)]
-        pltpu.make_async_copy(part, part, a_send.at[shard]).wait()
+        for chunk in range(CHUNKS):
+            sent_rows = send_a.at[shard, chunk, pl.ds(0, peers_rows)]
+            pltpu.make_async_copy(sent_rows, sent_rows, a_send.at[shard, chunk]).wait()
         for way in range(2):
             sent = has_next(way) & ((shard <= hid) if way == 0 else (shard >= hid))
 
             @pl.when(sent)
             def _():
-                line_copy(raw.at[shard], raw.at[shard], raw_send, raw_recv, way, shard).wait_send()
-                line_copy(routed_b.at[shard], routed_b.at[shard], rb_send, rb_recv, way, shard).wait_send()
-
-    part = send_b.at[pl.ds(0, peers_rows)]
-    pltpu.make_async_copy(part, part, b_send).wait()
+                for chunk in range(CHUNKS):
+                    raw_copy(way, shard, chunk).wait_send()
+                routed_copy(way, shard).wait_send()
+
+    sent_rows = send_b.at[pl.ds(0, peers_rows)]
+    pltpu.make_async_copy(sent_rows, sent_rows, b_send).wait()
     pltpu.make_async_copy(cnts.at[pl.ds(0, n_ex - 1)], cnts.at[pl.ds(0, n_ex - 1)], cnt_send).wait()
     for i in range(1, n_hid):
         meta_copy(i).wait_send()
@@ -332,7 +387,8 @@
     hidden = w_down.shape[1]
     slots = -(-slot_token.shape[2] // 16) * 16
     lanes = -(-2 * n_ex // 128) * 128
-    wide = features * 3 // 4 // TILE * TILE
+    wide = features * 3 // 4 // (CHUNKS * TILE) * CHUNKS * TILE
+    part = wide // CHUNKS
     narrow = features - wide
     group = CF * tokens
     dma = pltpu.SemaphoreType.DMA
@@ -347,27 +403,28 @@
             pltpu.VMEM(cotangent.shape, bf16),
             pltpu.VMEM(slot_token.shape, jnp.int32),
             pltpu.VMEM(slot_gate.shape, f32),
-            pltpu.VMEM((n_ex * slots, tokens), bf16),
-            pltpu.VMEM((n_ex * slots, TILE), f32),
+            pltpu.VMEM((n_hid, n_ex * slots, tokens), bf16),
+            pltpu.VMEM((n_hid, n_ex * slots, 128), f32),
             pltpu.VMEM((n_hid, group, n_ex * slots), bf16),
             pltpu.VMEM((features, hidden), bf16),
-            pltpu.VMEM((n_hid, tokens, wide), bf16),
+            pltpu.VMEM((group, hidden), f32),
+            pltpu.VMEM((n_hid, CHUNKS, tokens, part), bf16),
             pltpu.VMEM((lanes, 128), f32),
             pltpu.VMEM((n_hid, slots, lanes), f32),
             pltpu.VMEM((-(-n_hid // 8) * 8, lanes), f32),
             pltpu.VMEM((n_ex, -(-n_hid // 8) * 8, lanes), f32),
-            pltpu.VMEM((n_hid, n_ex * slots, wide), bf16),
+            pltpu.VMEM((n_hid, CHUNKS, n_ex * slots, part), bf16),
             pltpu.VMEM((n_ex * slots, narrow), bf16),
-            pltpu.VMEM((n_hid, n_ex * slots, wide), bf16),
+            pltpu.VMEM((n_hid, CHUNKS, n_ex * slots, part), bf16),
             pltpu.VMEM((n_ex * slots, narrow), bf16),
             pltpu.VMEM((n_hid, group, narrow), bf16),
-            pltpu.VMEM((group, wide), bf16),
-            pltpu.VMEM((hidden, features), bf16),
-            dma((2, n_hid)), dma((n_hid,)), dma((n_hid,)), dma((n_hid,)), dma, dma,
-            dma((n_hid,)), dma((n_hid,)), dma, dma, dma((2, n_hid)), dma((n_hid,)), dma((4,)),
+            pltpu.VMEM((group, part), bf16),
+            pltpu.VMEM((2, TILE, features), bf16),
+            dma((2, n_hid, CHUNKS)), dma((n_hid, CHUNKS)), dma((n_hid,)), dma((n_hid,)), dma, dma,
+            dma((n_hid, CHUNKS)), dma((n_hid, CHUNKS)), dma, dma, dma((2, n_hid)), dma((n_hid,)), dma((5,)),
         ],
         compiler_params=pltpu.CompilerParams(
-            collective_id=0, has_side_effects=True, vmem_limit_bytes=52 * 1024 * 1024
+            collective_id=0, has_side_effects=True, vmem_limit_bytes=56 * 1024 * 1024
         ),
         cost_estimate=pl.CostEstimate(
             flops=2 * n_hid * group * hidden * features, bytes_accessed=2 * hidden * features * 3, transcendentals=0

time: 123 us -> 123 us (level)
  no operation moved by 1% of the time
where the time goes in v4:
time: 123 us
  Pallas kernels  120 us (98%)
  local copies, waits for them, and re-layouts  2.02 us (2%)
    pallas_call x1, Pallas kernels, shards(): pl.pallas_call(functools.partial(kernel, n_ex, n_hid, slots), out_shape=p...  120 us

profile of v4, /device:TPU:0, one launch (start us, length us, event | category | flops | bytes accessed | tf_op | source)
XLA Modules:
  0.0 122.5 jit_solution(15586775180460987959)
XLA Ops:
  0.0 120.5 %route_and_multiply.1 = bf16[1,2048,1024]{2,1,0:T(8,128)(2,1)S(1)} custom-call(bf16[256,2048]{1,0:T(8,128)(2,1)} %cot_hbm.1, s32[1,8,80]{2,1,0:T(8,128)} %token_hbm.1, f32[1,8,80]{2,1,0:T(8,128)} %gate_hbm.1, bf16[1,1024,2048]{2,1,0:T(8,128)(2,1)} %w_hbm.1), custom_call_target="tpu_custom_call" | custom-call | flops 8589934592 | bytes 12582912 | tf_op jit(solution)/shard_map/route_and_multiply/pallas_call | solution.py:397
  120.5 2.0 %copy.6 = bf16[1,2048,1024]{2,1,0:T(8,128)(2,1)} copy(bf16[1,2048,1024]{2,1,0:T(8,128)(2,1)S(1)} %route_and_multiply.1) | data formatting | bytes 8388608

commit v5 on v4

--- a/solution.py
+++ b/solution.py
@@ -9,12 +9,17 @@
 
 CF = 2
 CHUNKS = 2
+RAW_SHARE = 11, 16
 TILE = 256
 MESH = pl.DeviceIdType.MESH
 
 
+def tile_of(width):
+    return width if width <= 640 else TILE if width % TILE == 0 else 128
+
+
 def kernel(
-    n_ex, n_hid, slots, cot_hbm, token_hbm, gate_hbm, w_hbm, stage,
+    n_ex, n_hid, slots, widths, cot_hbm, token_hbm, gate_hbm, w_hbm, stage,
     cot, token_in, gate_in, pick, gates, put, weight_t, total,
     raw, table, meta, cnt, cnts, send_a, send_b, got_a, got_b, routed_b, routed_a, weight,
     raw_send, raw_recv, meta_send, meta_recv, cnt_send, cnt_recv,
@@ -22,8 +27,8 @@
 ):
     ex, hid = lax.axis_index("expert"), lax.axis_index("hidden")
     tokens = cot.shape[0]
-    part = raw.shape[3]
-    wide = CHUNKS * part
+    starts = [sum(widths[:chunk]) for chunk in range(CHUNKS)]
+    wide = sum(widths)
     narrow = send_b.shape[1]
     group = routed_b.shape[1]
     lanes = meta.shape[2]
@@ -76,8 +81,8 @@
         )
 
     def raw_copy(way, shard, chunk, own=False):
-        held = raw.at[shard, chunk]
-        src = cot_hbm.at[:, pl.ds(chunk * part, part)] if own else held
+        held = raw.at[shard, chunk, :, pl.ds(0, widths[chunk])]
+        src = cot_hbm.at[:, pl.ds(starts[chunk], widths[chunk])] if own else held
         return to_next(src, held, raw_send.at[way, shard, chunk], raw_recv.at[shard, chunk], way)
 
     def routed_copy(way, shard):
@@ -127,21 +132,24 @@
 
         lax.fori_loop(0, n_ex, one, 0)
 
+    def tile(c, base=0, size=TILE):
+        return pl.ds(pl.multiple_of(base + c * size, 128), size)
+
     def scale(shard, rows, store, columns):
+        size = tile_of(columns)
+
         def one(c, carry):
-            rows_c = jnp.dot(pick[shard], rows(c), preferred_element_type=jnp.float32)
-            gate = jnp.concatenate([gates[shard]] * (TILE // 128), axis=1)
-            store(c, (gate * rows_c).astype(jnp.bfloat16))
-            return carry
-
-        lax.fori_loop(0, columns // TILE, one, 0)
-
-    def tile(c, base=0):
-        return pl.ds(pl.multiple_of(base + c * TILE, TILE), TILE)
+            rows_c = jnp.dot(pick[shard], rows(c, size), preferred_element_type=jnp.float32)
+            gate = jnp.concatenate([gates[shard]] * (size // 128), axis=1)
+            store(c, size, (gate * rows_c).astype(jnp.bfloat16))
+            return carry
+
+        lax.fori_loop(0, columns // size, one, 0)
 
     def a_copy(shard, chunk, expert):
         return pltpu.make_async_remote_copy(
-            src_ref=send_a.at[shard, chunk, rows_of(expert)], dst_ref=got_a.at[shard, chunk, rows_of(ex)],
+            src_ref=send_a.at[shard, chunk, rows_of(expert), pl.ds(0, widths[chunk])],
+            dst_ref=got_a.at[shard, chunk, rows_of(ex), pl.ds(0, widths[chunk])],
             send_sem=a_send.at[shard, chunk], recv_sem=a_recv.at[shard, chunk],
             device_id={"expert": expert}, device_id_type=MESH,
         )
@@ -152,8 +160,8 @@
             send_sem=b_send, recv_sem=b_recv, device_id={"expert": expert}, device_id_type=MESH,
         )
 
-    def store_narrow(c, value):
-        send_b[:, tile(c)] = value
+    def store_narrow(c, size, value):
+        send_b[:, tile(c, 0, size)] = value
 
     def start_narrow(i, carry):
         b_copy(lax.rem(ex + i, n_ex)).start()
@@ -161,24 +169,25 @@
 
     choose(hid)
     loads[2].wait()
-    scale(hid, lambda c: cot[:, tile(c, wide)], store_narrow, narrow)
+    scale(hid, lambda c, size: cot[:, tile(c, wide, size)], store_narrow, narrow)
     lax.fori_loop(1, n_ex, start_narrow, 0)
     got_b[rows_of(ex), :] = send_b[rows_of(ex), :]
 
     def send_wide(shard, chunk, rows):
-        def store_wide(c, value):
-            send_a[shard, chunk, :, tile(c)] = value
+        def store_wide(c, size, value):
+            send_a[shard, chunk, :, tile(c, 0, size)] = value
 
         def start_wide(i, carry):
             a_copy(shard, chunk, lax.rem(ex + i, n_ex)).start()
             return carry
 
-        scale(shard, rows, store_wide, part)
+        scale(shard, rows, store_wide, widths[chunk])
         lax.fori_loop(1, n_ex, start_wide, 0)
-        got_a[shard, chunk, rows_of(ex), :] = send_a[shard, chunk, rows_of(ex), :]
+        own = slice(0, widths[chunk])
+        got_a[shard, chunk, rows_of(ex), own] = send_a[shard, chunk, rows_of(ex), own]
 
     for chunk in range(CHUNKS):
-        send_wide(hid, chunk, lambda c: cot[:, tile(c, chunk * part)])
+        send_wide(hid, chunk, lambda c, size: cot[:, tile(c, starts[chunk], size)])
 
     for i in range(1, n_hid):
         source = lax.rem(hid + i, n_hid)
@@ -243,13 +252,14 @@
         both_ways(one)
 
     def take_raw(way, shard, chunk):
-        pltpu.make_async_copy(raw.at[shard, chunk], raw.at[shard, chunk], raw_recv.at[shard, chunk]).wait()
+        held = raw.at[shard, chunk, :, pl.ds(0, widths[chunk])]
+        pltpu.make_async_copy(held, held, raw_recv.at[shard, chunk]).wait()
 
         @pl.when(has_next(way))
         def _():
             raw_copy(way, shard, chunk).start()
 
-        send_wide(shard, chunk, lambda c: raw[shard, chunk, :, tile(c)])
+        send_wide(shard, chunk, lambda c, size: raw[shard, chunk, :, tile(c, 0, size)])
 
     def take_routed(way, shard):
         pltpu.make_async_copy(routed_b.at[shard], routed_b.at[shard], rb_recv.at[shard]).wait()
@@ -294,15 +304,17 @@
 
     def compact(shard, chunk):
         if n_ex > 1:
-            arrived = got_a.at[shard, chunk, pl.ds(0, peers_rows)]
+            arrived = got_a.at[shard, chunk, pl.ds(0, peers_rows), pl.ds(0, widths[chunk])]
             pltpu.make_async_copy(arrived, arrived, a_recv.at[shard, chunk]).wait()
 
         def one(c, carry):
-            rows = jnp.dot(put[shard], got_a[shard, chunk, :, tile(c)], preferred_element_type=jnp.float32)
-            routed_a[:, tile(c)] = rows.astype(jnp.bfloat16)
-            return carry
-
-        lax.fori_loop(0, part // TILE, one, 0)
+            columns = tile(c, 0, size)
+            rows = jnp.dot(put[shard], got_a[shard, chunk, :, columns], preferred_element_type=jnp.float32)
+            routed_a[:, columns] = rows.astype(jnp.bfloat16)
+            return carry
+
+        size = tile_of(widths[chunk])
+        lax.fori_loop(0, widths[chunk] // size, one, 0)
 
     def over_columns(body):
         def one(c, carry):
@@ -316,7 +328,7 @@
             compact(shard, chunk)
 
             def add(columns, chunk=chunk):
-                value = product(routed_a[...], chunk * part, columns)
+                value = product(routed_a[:, : widths[chunk]], starts[chunk], columns)
                 total[:, columns] = value if chunk == 0 else total[:, columns] + value
 
             over_columns(add)
@@ -333,7 +345,7 @@
         rows = pl.ds(pl.multiple_of(shard * group, 16), group)
 
         def write(columns):
-            value = total[:, columns] + product(routed_a[...], (CHUNKS - 1) * part, columns)
+            value = total[:, columns] + product(routed_a[:, : widths[-1]], starts[-1], columns)
             stage[0, rows, columns] = value.astype(jnp.bfloat16)
 
         over_columns(write)
@@ -364,7 +376,7 @@
 
     for shard in range(n_hid):
         for chunk in range(CHUNKS):
-            sent_rows = send_a.at[shard, chunk, pl.ds(0, peers_rows)]
+            sent_rows = send_a.at[shard, chunk, pl.ds(0, peers_rows), pl.ds(0, widths[chunk])]
             pltpu.make_async_copy(sent_rows, sent_rows, a_send.at[shard, chunk]).wait()
         for way in range(2):
             sent = has_next(way) & ((shard <= hid) if way == 0 else (shard >= hid))
@@ -387,15 +399,16 @@
     hidden = w_down.shape[1]
     slots = -(-slot_token.shape[2] // 16) * 16
     lanes = -(-2 * n_ex // 128) * 128
-    wide = features * 3 // 4 // (CHUNKS * TILE) * CHUNKS * TILE
-    part = wide // CHUNKS
+    wide = features * RAW_SHARE[0] // RAW_SHARE[1] // 128 * 128
+    part = -(-wide // (128 * CHUNKS)) * 128
+    widths = tuple(min(part, wide - chunk * part) for chunk in range(CHUNKS))
     narrow = features - wide
     group = CF * tokens
     dma = pltpu.SemaphoreType.DMA
     bf16, f32 = jnp.bfloat16, jnp.float32
     hbm = pl.BlockSpec(memory_space=pltpu.HBM)
     return pl.pallas_call(
-        functools.partial(kernel, n_ex, n_hid, slots),
+        functools.partial(kernel, n_ex, n_hid, slots, widths),
         out_shape=pltpu.VMEM((1, n_hid * group, hidden), bf16),
         in_specs=[hbm, hbm, hbm, hbm],
         out_specs=pl.BlockSpec(memory_space=pltpu.VMEM),

time: 123 us -> 128 us (1.041)
  Pallas kernels: 120 us -> 126 us
    pallas_call x1, Pallas kernels: 120 us -> 126 us  [shards(): pl.pallas_call(functools.partial(kernel, n_ex, n_hid, slots, widths), out...]
where the time goes in v5:
time: 128 us
  Pallas kernels  126 us (98%)
  local copies, waits for them, and re-layouts  2.02 us (2%)
    pallas_call x1, Pallas kernels, shards(): pl.pallas_call(functools.partial(kernel, n_ex, n_hid, slots, widths), out...  126 us

profile of v5, /device:TPU:0, one launch (start us, length us, event | category | flops | bytes accessed | tf_op | source)
XLA Modules:
  0.0 128.2 jit_solution(1088539127009730086)
XLA Ops:
  0.0 126.1 %route_and_multiply.1 = bf16[1,2048,1024]{2,1,0:T(8,128)(2,1)S(1)} custom-call(bf16[256,2048]{1,0:T(8,128)(2,1)} %cot_hbm.1, s32[1,8,80]{2,1,0:T(8,128)} %token_hbm.1, f32[1,8,80]{2,1,0:T(8,128)} %gate_hbm.1, bf16[1,1024,2048]{2,1,0:T(8,128)(2,1)} %w_hbm.1), custom_call_target="tpu_custom_call" | custom-call | flops 8589934592 | bytes 12582912 | tf_op jit(solution)/shard_map/route_and_multiply/pallas_call | solution.py:410
  126.1 2.0 %copy.6 = bf16[1,2048,1024]{2,1,0:T(8,128)(2,1)} copy(bf16[1,2048,1024]{2,1,0:T(8,128)(2,1)S(1)} %route_and_multiply.1) | data formatting | bytes 8388608

commit v6 on v5

--- a/solution.py
+++ b/solution.py
@@ -9,7 +9,7 @@
 
 CF = 2
 CHUNKS = 2
-RAW_SHARE = 11, 16
+RAW_SHARE = 13, 16
 TILE = 256
 MESH = pl.DeviceIdType.MESH
 
@@ -27,6 +27,9 @@
 ):
     ex, hid = lax.axis_index("expert"), lax.axis_index("hidden")
     tokens = cot.shape[0]
+    def span(chunk):
+        return pl.ds(starts[chunk], widths[chunk])
+
     starts = [sum(widths[:chunk]) for chunk in range(CHUNKS)]
     wide = sum(widths)
     narrow = send_b.shape[1]
@@ -81,7 +84,7 @@
         )
 
     def raw_copy(way, shard, chunk, own=False):
-        held = raw.at[shard, chunk, :, pl.ds(0, widths[chunk])]
+        held = raw.at[shard, :, span(chunk)]
         src = cot_hbm.at[:, pl.ds(starts[chunk], widths[chunk])] if own else held
         return to_next(src, held, raw_send.at[way, shard, chunk], raw_recv.at[shard, chunk], way)
 
@@ -148,8 +151,8 @@
 
     def a_copy(shard, chunk, expert):
         return pltpu.make_async_remote_copy(
-            src_ref=send_a.at[shard, chunk, rows_of(expert), pl.ds(0, widths[chunk])],
-            dst_ref=got_a.at[shard, chunk, rows_of(ex), pl.ds(0, widths[chunk])],
+            src_ref=send_a.at[shard, rows_of(expert), span(chunk)],
+            dst_ref=got_a.at[shard, rows_of(ex), span(chunk)],
             send_sem=a_send.at[shard, chunk], recv_sem=a_recv.at[shard, chunk],
             device_id={"expert": expert}, device_id_type=MESH,
         )
@@ -175,7 +178,7 @@
 
     def send_wide(shard, chunk, rows):
         def store_wide(c, size, value):
-            send_a[shard, chunk, :, tile(c, 0, size)] = value
+            send_a[shard, :, tile(c, starts[chunk], size)] = value
 
         def start_wide(i, carry):
             a_copy(shard, chunk, lax.rem(ex + i, n_ex)).start()
@@ -183,8 +186,7 @@
 
         scale(shard, rows, store_wide, widths[chunk])
         lax.fori_loop(1, n_ex, start_wide, 0)
-        own = slice(0, widths[chunk])
-        got_a[shard, chunk, rows_of(ex), own] = send_a[shard, chunk, rows_of(ex), own]
+        got_a[shard, rows_of(ex), span(chunk)] = send_a[shard, rows_of(ex), span(chunk)]
 
     for chunk in range(CHUNKS):
         send_wide(hid, chunk, lambda c, size: cot[:, tile(c, starts[chunk], size)])
@@ -252,14 +254,14 @@
         both_ways(one)
 
     def take_raw(way, shard, chunk):
-        held = raw.at[shard, chunk, :, pl.ds(0, widths[chunk])]
+        held = raw.at[shard, :, span(chunk)]
         pltpu.make_async_copy(held, held, raw_recv.at[shard, chunk]).wait()
 
         @pl.when(has_next(way))
         def _():
             raw_copy(way, shard, chunk).start()
 
-        send_wide(shard, chunk, lambda c, size: raw[shard, chunk, :, tile(c, 0, size)])
+        send_wide(shard, chunk, lambda c, size: raw[shard, :, tile(c, starts[chunk], size)])
 
     def take_routed(way, shard):
         pltpu.make_async_copy(routed_b.at[shard], routed_b.at[shard], rb_recv.at[shard]).wait()
@@ -304,12 +306,12 @@
 
     def compact(shard, chunk):
         if n_ex > 1:
-            arrived = got_a.at[shard, chunk, pl.ds(0, peers_rows), pl.ds(0, widths[chunk])]
+            arrived = got_a.at[shard, pl.ds(0, peers_rows), span(chunk)]
             pltpu.make_async_copy(arrived, arrived, a_recv.at[shard, chunk]).wait()
 
         def one(c, carry):
             columns = tile(c, 0, size)
-            rows = jnp.dot(put[shard], got_a[shard, chunk, :, columns], preferred_element_type=jnp.float32)
+            rows = jnp.dot(put[shard], got_a[shard, :, tile(c, starts[chunk], size)], preferred_element_type=jnp.float32)
             routed_a[:, columns] = rows.astype(jnp.bfloat16)
             return carry
 
@@ -356,9 +358,7 @@
             take_routed(way, shard)
 
     def along_routed(step, carry):
-        @pl.when(step > 0)
-        def _():
-            on_line(step, take_to_pass)
+        on_line(step + 1, take_to_pass)
 
         def one(way, inner):
             shard = hid - step + 2 * step * way
@@ -376,7 +376,7 @@
 
     for shard in range(n_hid):
         for chunk in range(CHUNKS):
-            sent_rows = send_a.at[shard, chunk, pl.ds(0, peers_rows), pl.ds(0, widths[chunk])]
+            sent_rows = send_a.at[shard, pl.ds(0, peers_rows), span(chunk)]
             pltpu.make_async_copy(sent_rows, sent_rows, a_send.at[shard, chunk]).wait()
         for way in range(2):
             sent = has_next(way) & ((shard <= hid) if way == 0 else (shard >= hid))
@@ -400,7 +400,7 @@
     slots = -(-slot_token.shape[2] // 16) * 16
     lanes = -(-2 * n_ex // 128) * 128
     wide = features * RAW_SHARE[0] // RAW_SHARE[1] // 128 * 128
-    part = -(-wide // (128 * CHUNKS)) * 128
+    part = -(-wide // (TILE * CHUNKS)) * TILE
     widths = tuple(min(part, wide - chunk * part) for chunk in range(CHUNKS))
     narrow = features - wide
     group = CF * tokens
@@ -421,14 +421,14 @@
             pltpu.VMEM((n_hid, group, n_ex * slots), bf16),
             pltpu.VMEM((features, hidden), bf16),
             pltpu.VMEM((group, hidden), f32),
-            pltpu.VMEM((n_hid, CHUNKS, tokens, part), bf16),
+            pltpu.VMEM((n_hid, tokens, wide), bf16),
             pltpu.VMEM((lanes, 128), f32),
             pltpu.VMEM((n_hid, slots, lanes), f32),
             pltpu.VMEM((-(-n_hid // 8) * 8, lanes), f32),
             pltpu.VMEM((n_ex, -(-n_hid // 8) * 8, lanes), f32),
-            pltpu.VMEM((n_hid, CHUNKS, n_ex * slots, part), bf16),
+            pltpu.VMEM((n_hid, n_ex * slots, wide), bf16),
             pltpu.VMEM((n_ex * slots, narrow), bf16),
-            pltpu.VMEM((n_hid, CHUNKS, n_ex * slots, part), bf16),
+            pltpu.VMEM((n_hid, n_ex * slots, wide), bf16),
             pltpu.VMEM((n_ex * slots, narrow), bf16),
             pltpu.VMEM((n_hid, group, narrow), bf16),
             pltpu.VMEM((group, part), bf16),

time: 128 us -> 122 us (0.953); the launches traced: 128 us -> 121 us
  Pallas kernels: 126 us -> 118 us
    pallas_call x1, Pallas kernels: 126 us -> 118 us  [shards(): pl.pallas_call(functools.partial(kernel, n_ex, n_hid, slots, widths), out...]
where the time goes in v6:
time: 122 us; the launch traced here: 121 us
  Pallas kernels  118 us (97%)
  local copies, waits for them, and re-layouts  2.02 us (2%)
    pallas_call x1, Pallas kernels, shards(): pl.pallas_call(functools.partial(kernel, n_ex, n_hid, slots, widths), out...  118 us

profile of v6, /device:TPU:0, one launch (start us, length us, event | category | flops | bytes accessed | tf_op | source)
XLA Modules:
  0.0 120.5 jit_solution(18403941177042712754)
XLA Ops:
  0.0 118.5 %route_and_multiply.1 = bf16[1,2048,1024]{2,1,0:T(8,128)(2,1)S(1)} custom-call(bf16[256,2048]{1,0:T(8,128)(2,1)} %cot_hbm.1, s32[1,8,80]{2,1,0:T(8,128)} %token_hbm.1, f32[1,8,80]{2,1,0:T(8,128)} %gate_hbm.1, bf16[1,1024,2048]{2,1,0:T(8,128)(2,1)} %w_hbm.1), custom_call_target="tpu_custom_call" | custom-call | flops 8589934592 | bytes 12582912 | tf_op jit(solution)/shard_map/route_and_multiply/pallas_call | solution.py:410
  118.5 2.0 %copy.6 = bf16[1,2048,1024]{2,1,0:T(8,128)(2,1)} copy(bf16[1,2048,1024]{2,1,0:T(8,128)(2,1)S(1)} %route_and_multiply.1) | data formatting | bytes 8388608

commit v7 on v6

--- a/solution.py
+++ b/solution.py
@@ -9,7 +9,7 @@
 
 CF = 2
 CHUNKS = 2
-RAW_SHARE = 13, 16
+RAW_SHARE = 12, 16
 TILE = 256
 MESH = pl.DeviceIdType.MESH
 
@@ -69,7 +69,6 @@
 
     lax.fori_loop(1, n_ex, greet_plane, 0)
     lax.fori_loop(1, n_hid, greet_line, 0)
-    pl.semaphore_wait(barrier, n_ex + n_hid - 2)
 
     def meta_copy(i):
         return pltpu.make_async_remote_copy(
@@ -108,8 +107,6 @@
         def _():
             raw_copy(way, hid, chunk, own=True).start()
 
-    for chunk in range(CHUNKS):
-        both_ways(functools.partial(start_raw, chunk=chunk))
     loads[0].wait()
     loads[1].wait()
     live_slots = token_in.shape[2]
@@ -117,8 +114,6 @@
     table[0:n_ex, 0:live_slots] = token_in[0].astype(jnp.float32)
     table[n_ex : 2 * n_ex, 0:live_slots] = gate_in[0]
     meta[hid] = table[...].T[0:slots, :]
-    for i in range(1, n_hid):
-        meta_copy(i).start()
 
     lane = lax.broadcasted_iota(jnp.int32, (slots, lanes), 1)
     token_iota = lax.broadcasted_iota(jnp.int32, (slots, tokens), 1).astype(jnp.float32)
@@ -171,6 +166,11 @@
         return carry
 
     choose(hid)
+    pl.semaphore_wait(barrier, n_ex + n_hid - 2)
+    for chunk in range(CHUNKS):
+        both_ways(functools.partial(start_raw, chunk=chunk))
+    for i in range(1, n_hid):
+        meta_copy(i).start()
     loads[2].wait()
     scale(hid, lambda c, size: cot[:, tile(c, wide, size)], store_narrow, narrow)
     lax.fori_loop(1, n_ex, start_narrow, 0)

time: 122 us -> 122 us (level)
  no operation moved by 1% of the time
where the time goes in v7:
time: 122 us; the launch traced here: 121 us
  Pallas kernels  119 us (98%)
  local copies, waits for them, and re-layouts  2.02 us (2%)
    pallas_call x1, Pallas kernels, shards(): pl.pallas_call(functools.partial(kernel, n_ex, n_hid, slots, widths), out...  119 us

profile of v7, /device:TPU:0, one launch (start us, length us, event | category | flops | bytes accessed | tf_op | source)
XLA Modules:
  0.0 121.5 jit_solution(18067316290531171157)
XLA Ops:
  0.0 119.4 %route_and_multiply.1 = bf16[1,2048,1024]{2,1,0:T(8,128)(2,1)S(1)} custom-call(bf16[256,2048]{1,0:T(8,128)(2,1)} %cot_hbm.1, s32[1,8,80]{2,1,0:T(8,128)} %token_hbm.1, f32[1,8,80]{2,1,0:T(8,128)} %gate_hbm.1, bf16[1,1024,2048]{2,1,0:T(8,128)(2,1)} %w_hbm.1), custom_call_target="tpu_custom_call" | custom-call | flops 8589934592 | bytes 12582912 | tf_op jit(solution)/shard_map/route_and_multiply/pallas_call | solution.py:410
  119.4 2.0 %copy.6 = bf16[1,2048,1024]{2,1,0:T(8,128)(2,1)} copy(bf16[1,2048,1024]{2,1,0:T(8,128)(2,1)S(1)} %route_and_multiply.1) | data formatting | bytes 8388608
